TPU v7x, 512 devices: a whole 4x4x16 slice. The times are simulated.
512 devices in a mesh: dp: 16 (over z_lo, core), ctx: 32 (over y, z_hi, x).
Axes of the slice: x: 4, y: 4, z: 16 (z_hi: 2, z_lo: 8; z = z_hi * 8 + z_lo), core: 2. Of those that a mesh axis runs over, the one named last changes fastest.
Arguments:
- features: bfloat16 [16, 4096, 4096], P('dp', 'ctx'), may hold values from -6 to 6
- cotangent: bfloat16 [16, 4096, 4096], P('dp', 'ctx'), may hold values from -6 to 6
- filters: bfloat16 [256, 128], replicated, may hold values from -0.5 to 0.5
- skip_gain: float32 [4096], replicated, may hold values from -3 to 3
Outputs:
- conv_out: bfloat16 [16, 4096, 4096], P('dp', 'ctx')
- grad_input: bfloat16 [16, 4096, 4096], P('dp', 'ctx')
- grad_filters: float32 [256, 128], P('ctx', 'dp')
- grad_skip: float32 [4096], P(('ctx', 'dp'))
All inputs are finite; a program needn't handle non-finite values.
Results may differ from a plain program's by a relative error of at most 0.001.
Values may be sent and summed in bfloat16 or wider, within the bound.
No kernel may reach another device: no remote copies, remote signals or barrier semaphores. Data moves between devices by JAX's collectives and lax.ppermute only.
A program may use at most 64 MiB of HBM per device.

v0:
```python
import math

import jax
import jax.numpy as jnp
from jax import lax
from jax.experimental import pallas as pl
from jax.experimental.pallas import tpu as pltpu
from jax.sharding import PartitionSpec as P

CH = 16
TAPS = 128
LANES = 128
PER = LANES // CH
HALF = 64
QUARTER = 32
TILES = 4
VMEM = 48 * 1024 * 1024


def params():
    return pltpu.CompilerParams(vmem_limit_bytes=VMEM)


def rolled(row, count):
    wide = jnp.broadcast_to(row, (count, row.shape[1]))
    return pltpu.roll(wide, 0, 1, stride=1, stride_axis=0)


def toeplitz_kernel(taps_ref, fwd_in_ref, fwd_across_ref, bwd_in_ref, bwd_across_ref):
    taps = taps_ref[...]
    source = lax.broadcasted_iota(jnp.int32, (TAPS, 2 * TAPS), 0)
    target = lax.broadcasted_iota(jnp.int32, (TAPS, 2 * TAPS), 1)
    turn = jnp.where(source + target == TAPS, 1.0, 0.0).astype(jnp.bfloat16)
    place = jnp.where(source == target, 1.0, 0.0).astype(jnp.bfloat16)
    back = jnp.dot(taps, turn, preferred_element_type=jnp.float32)
    ahead = jnp.dot(taps, place, preferred_element_type=jnp.float32)
    for group in range(taps.shape[0]):
        rows = pl.ds(group * HALF, HALF)
        fwd = rolled(back[group : group + 1], HALF)
        fwd_across_ref[rows] = fwd[:, :TAPS].astype(jnp.bfloat16)
        fwd_in_ref[rows] = fwd[:, HALF : HALF + TAPS].astype(jnp.bfloat16)
        bwd = rolled(ahead[group : group + 1], HALF)
        bwd_in_ref[rows] = bwd[:, :TAPS].astype(jnp.bfloat16)
        bwd_across_ref[rows] = bwd[:, HALF : HALF + TAPS].astype(jnp.bfloat16)


def toeplitz(filters):
    groups = filters.shape[0]
    step = TILES * PER
    shape = jax.ShapeDtypeStruct((groups * HALF, TAPS), jnp.bfloat16)
    return pl.pallas_call(
        toeplitz_kernel,
        grid=(groups // step,),
        in_specs=[pl.BlockSpec((step, TAPS), lambda i: (i, 0))],
        out_specs=[pl.BlockSpec((step * HALF, TAPS), lambda i: (i, 0))] * 4,
        out_shape=[shape] * 4,
        compiler_params=params(),
        name="toeplitz",
    )(filters)


def head_window(block):
    return jnp.concatenate([block, jnp.concatenate([block[HALF:], jnp.zeros_like(block[HALF:])], axis=0)], axis=1)


def tail_window(block):
    return jnp.concatenate([jnp.concatenate([jnp.zeros_like(block[:HALF]), block[:HALF]], axis=0), block], axis=1)


def picked(product):
    lane = lax.broadcasted_iota(jnp.int32, (HALF, 2 * LANES), 1)
    owner = (lane % LANES) // CH
    kept = product[:HALF]
    for group in range(1, PER):
        kept = jnp.where(owner == group, product[group * HALF : (group + 1) * HALF], kept)
    return jnp.concatenate([kept[:, :LANES], kept[:, LANES:]], axis=0)


def convolved(matrix, window):
    return picked(jnp.dot(matrix, window, preferred_element_type=jnp.float32))


def tile_of(index):
    return slice(index * LANES, (index + 1) * LANES), slice(index * PER * HALF, (index + 1) * PER * HALF)


def local_kernel(cur_ref, grad_ref, fwd_ref, bwd_ref, skip_ref, fwd_out_ref, bwd_out_ref, diag_ref):
    for index in range(TILES):
        lanes, rows = tile_of(index)
        cur, grad, skip = cur_ref[:, lanes], grad_ref[:, lanes], skip_ref[:, lanes]
        cur_wide, grad_wide = cur.astype(jnp.float32), grad.astype(jnp.float32)
        fwd_out_ref[:, lanes] = convolved(fwd_ref[rows], tail_window(cur)) + skip * cur_wide
        bwd_out_ref[:, lanes] = convolved(bwd_ref[rows], head_window(grad)) + skip * grad_wide
        diag_ref[:, lanes] = jnp.sum(cur_wide * grad_wide, axis=0, keepdims=True)


def chan_spec(rows):
    return pl.BlockSpec((rows, TILES * LANES), lambda i: (0, i))


def matrix_spec():
    return pl.BlockSpec((TILES * PER * HALF, TAPS), lambda i: (i, 0))


def local_part(cur, grad, fwd_in, bwd_in, skip):
    tokens, chans = cur.shape
    wide = jax.ShapeDtypeStruct((tokens, chans), jnp.float32)
    return pl.pallas_call(
        local_kernel,
        grid=(chans // (TILES * LANES),),
        in_specs=[chan_spec(tokens), chan_spec(tokens), matrix_spec(), matrix_spec(), chan_spec(1)],
        out_specs=[chan_spec(tokens), chan_spec(tokens), chan_spec(1)],
        out_shape=[wide, wide, jax.ShapeDtypeStruct((1, chans), jnp.float32)],
        compiler_params=params(),
        name="local_part",
    )(cur, grad, fwd_in, bwd_in, skip)


def across_kernel(window, part_ref, halo_ref, matrix_ref, out_ref):
    for index in range(TILES):
        lanes, rows = tile_of(index)
        total = part_ref[:, lanes] + convolved(matrix_ref[rows], window(halo_ref[:, lanes]))
        out_ref[:, lanes] = total.astype(jnp.bfloat16)


def across_part(window, partial_sum, halo, matrix, name):
    tokens, chans = halo.shape
    return pl.pallas_call(
        lambda *refs: across_kernel(window, *refs),
        grid=(chans // (TILES * LANES),),
        in_specs=[chan_spec(tokens), chan_spec(tokens), matrix_spec()],
        out_specs=chan_spec(tokens),
        out_shape=jax.ShapeDtypeStruct((tokens, chans), jnp.bfloat16),
        compiler_params=params(),
        name=name,
    )(partial_sum, halo, matrix)


def lag_tile(earlier, cur, grad):
    both = jnp.concatenate([earlier, cur], axis=0)
    span = QUARTER + TAPS
    blocks = TAPS // QUARTER
    values = jnp.concatenate([both[b * QUARTER : b * QUARTER + span] for b in range(blocks)], axis=1)
    grads = jnp.concatenate([grad[b * QUARTER : (b + 1) * QUARTER] for b in range(blocks)], axis=1)
    lane = lax.broadcasted_iota(jnp.int32, grads.shape, 1)
    owner = (lane % LANES) // CH
    zero = jnp.zeros_like(grads)
    masked = jnp.concatenate([jnp.where(owner == group, grads, zero) for group in range(PER)], axis=0)
    cross = lax.dot_general(masked, values, (((1,), (1,)), ((), ())), preferred_element_type=jnp.float32)
    cross = jnp.concatenate([cross, jnp.zeros((cross.shape[0], 2 * TAPS - span), jnp.float32)], axis=1)
    rows = 8
    parts = cross.reshape(PER, QUARTER // rows, rows, 2 * TAPS)
    total = parts[:, 0].reshape(PER * rows, 2 * TAPS)
    for part in range(1, QUARTER // rows):
        moved = pltpu.roll(parts[:, part].reshape(PER * rows, 2 * TAPS), 2 * TAPS - part * rows, 1)
        total = total + moved
    row = lax.broadcasted_iota(jnp.int32, total.shape, 0) % rows
    for bit in (1, 2, 4):
        total = jnp.where(row & bit != 0, pltpu.roll(total, 2 * TAPS - bit, 1), total)
    return jnp.sum(total.reshape(PER, rows, 2 * TAPS), axis=1)


def lag_kernel(earlier_ref, cur_ref, grad_ref, out_ref):
    sums = []
    for index in range(TILES):
        lanes, _ = tile_of(index)
        sums.append(lag_tile(earlier_ref[:, lanes], cur_ref[:, lanes], grad_ref[:, lanes]))
    sums = jnp.concatenate(sums, axis=0)
    source = lax.broadcasted_iota(jnp.int32, (2 * TAPS, TAPS), 0)
    target = lax.broadcasted_iota(jnp.int32, (2 * TAPS, TAPS), 1)
    turn = jnp.where(source + target == TAPS, 1.0, 0.0)
    out_ref[...] = jnp.dot(sums, turn, precision=lax.Precision.HIGHEST, preferred_element_type=jnp.float32)


def lag_sums(earlier, cur, grad):
    tokens, chans = cur.shape
    return pl.pallas_call(
        lag_kernel,
        grid=(chans // (TILES * LANES),),
        in_specs=[chan_spec(tokens)] * 3,
        out_specs=pl.BlockSpec((TILES * PER, TAPS), lambda i: (i, 0)),
        out_shape=jax.ShapeDtypeStruct((chans // CH, TAPS), jnp.float32),
        compiler_params=params(),
        name="lag_sums",
    )(earlier, cur, grad)


def reduced(lagged, diagonal):
    ctx, dp = lax.axis_size("ctx"), lax.axis_size("dp")
    groups, chans = lagged.shape[0] // ctx, diagonal.shape[1] // ctx
    sent = jnp.concatenate([lagged.reshape(ctx, groups * TAPS), diagonal.reshape(ctx, chans)], axis=1)
    got = jnp.sum(lax.all_to_all(sent, "ctx", 0, 0, tiled=True), axis=0)
    taps = got[: groups * TAPS].reshape(groups, dp, TAPS // dp).transpose(1, 0, 2).reshape(dp, -1)
    sent = jnp.concatenate([taps, got[groups * TAPS :].reshape(dp, chans // dp)], axis=1)
    got = jnp.sum(lax.all_to_all(sent, "dp", 0, 0, tiled=True), axis=0)
    cut = groups * TAPS // dp
    return got[:cut].reshape(groups, TAPS // dp), got[cut:]


def shards(features, cotangent, filters, skip_gain):
    ctx = lax.axis_size("ctx")
    token_total = lax.axis_size("dp") * features.shape[0] * features.shape[1] * ctx
    cur, grad = features[0], cotangent[0]
    earlier = lax.ppermute(cur, "ctx", [(i, i + 1) for i in range(ctx - 1)])
    later = lax.ppermute(grad, "ctx", [(i + 1, i) for i in range(ctx - 1)])
    fwd_in, fwd_across, bwd_in, bwd_across = toeplitz(filters)
    fwd, bwd, diagonal = local_part(cur, grad, fwd_in, bwd_in, skip_gain.reshape(1, -1))
    lagged = lag_sums(earlier, cur, grad)
    conv_out = across_part(head_window, fwd, earlier, fwd_across, "fwd_across")
    grad_input = across_part(tail_window, bwd, later, bwd_across, "bwd_across")
    lagged, diagonal = reduced(lagged, diagonal)
    grad_filters = lagged / math.sqrt(token_total * CH)
    grad_skip = diagonal / math.sqrt(token_total)
    return (conv_out[None], grad_input[None], grad_filters, grad_skip)


def solution(mesh):
    return jax.shard_map(
        shards,
        mesh=mesh,
        in_specs=(P("dp", "ctx", None), P("dp", "ctx", None), P(), P()),
        out_specs=(P("dp", "ctx", None), P("dp", "ctx", None), P("ctx", "dp"), P(("ctx", "dp"))),
        check_vma=False,
    )
```

profile of v0, /device:TPU:1, one launch (start us, length us, event | category | flops | bytes accessed | tf_op | source)
XLA Modules:
  0.0 174.4 jit_solution(7337721575872514336)
XLA Ops:
  0.6 4.0 %collective-permute-start = (bf16[128,4096]{1,0:T(8,128)(2,1)}, bf16[128,4096]{1,0:T(8,128)(2,1)S(1)}, u32[]{:S(2)}, u32[]{:S(2)}) collective-permute-start(bf16[128,4096]{1,0:T(8,128)(2,1)} %bitcast.9), channel_id=1, source_target_pairs={{0,1},{1,2},{2,3},{3,4},{4,5},{5,6},{6,7},{7,8},{8,9},{9,10},{10,1... | collective-permute-start | bytes 3145736 | tf_op jit(solution)/shard_map/ppermute | solution.py:204
  4.7 1.3 collective-permute-start.1
  6.0 0.8 copy-done.4
  6.8 35.9 %toeplitz.1 = (bf16[16384,128]{1,0:T(8,128)(2,1)S(1)}, bf16[16384,128]{1,0:T(8,128)(2,1)}, bf16[16384,128]{1,0:T(8,128)(2,1)}, bf16[16384,128]{1,0:T(8,128)(2,1)}) custom-call(bf16[256,128]{1,0:T(8,128)(2,1)S(1)} %copy-done.4), custom_call_target="tpu_custom_call" | custom-call | tf_op jit(solution)/shard_map/toeplitz/pallas_call | solution.py:51
  42.7 1.9 %copy-done = bf16[16384,128]{1,0:T(8,128)(2,1)} copy-done((bf16[16384,128]{1,0:T(8,128)(2,1)}, bf16[16384,128]{1,0:T(8,128)(2,1)S(1)}, u32[]{:S(2)}) %copy-start) | copy-done | bytes 4194328
  44.7 1.2 copy-done.1
  45.9 1.2 copy-done.2
  47.1 0.7 copy-done.5
  47.8 9.9 %local_part.1 = (f32[128,4096]{1,0:T(8,128)S(1)}, f32[128,4096]{1,0:T(8,128)}, f32[1,4096]{1,0:T(1,128)S(1)}) custom-call(bf16[128,4096]{1,0:T(8,128)(2,1)S(1)} %bitcast.10, bf16[128,4096]{1,0:T(8,128)(2,1)S(1)} %bitcast.13, bf16[16384,128]{1,0:T(8,128)(2,1)} %copy-done, bf16[16384,128]{1,0:T(8,128)(2,1)} %get-tuple-element.12.bwd_ref, f32[1,4096]{1,0:T(1,128)S(1)} %bitcast.15), custom_call_target="tpu_custom_call" | custom-call | tf_op jit(solution)/shard_map/local_part/pallas_call | solution.py:108
  57.7 8.5 %lag_sums.1 = f32[256,128]{1,0:T(8,128)S(1)} custom-call(bf16[128,4096]{1,0:T(8,128)(2,1)S(1)} %collective-permute-done.refs_1_.earlier_ref, bf16[128,4096]{1,0:T(8,128)(2,1)S(1)} %bitcast.11, bf16[128,4096]{1,0:T(8,128)(2,1)S(1)} %bitcast.14), custom_call_target="tpu_custom_call" | custom-call | tf_op jit(solution)/shard_map/lag_sums/pallas_call | solution.py:177
  66.2 0.1 reshape.58
  66.3 0.1 all_to_all.12
  66.4 58.2 %all_to_all.18 = f32[32,1,1152]{2,1,0:T(1,128)S(1)} all-to-all(f32[32,1,1152]{2,1,0:T(1,128)S(1)} %all_to_all.12), channel_id=1, replica_groups=mesh['dp'=16,'ctx'=32] {'ctx'}, dimensions={0} | all-to-all | bytes 294912 | tf_op jit(solution)/shard_map/all_to_all | solution.py:192
  124.5 0.1 reduce_sum.18
  124.7 0.1 reshape.60
  124.8 0.1 copy.10
  124.8 0.1 copy.11
  124.9 0.1 reshape.62
  125.0 0.7 pad_maximum_fusion.1
  125.7 32.1 %all-to-all-start.1 = ((f32[16,1,72]{2,1,0:T(1,128)}), f32[16,1,72]{2,1,0:T(1,128)S(1)}, u32[]{:S(2)}, u32[]{:S(2)}) async-start(f32[16,1,72]{2,1,0:T(1,128)} %bitcast.8), calls=%async_computation.1 | async-start | bytes 16384 | tf_op jit(solution)/shard_map/all_to_all | solution.py:195
  157.8 7.6 %fwd_across.1 = bf16[128,4096]{1,0:T(8,128)(2,1)} custom-call(f32[128,4096]{1,0:T(8,128)S(1)} %get-tuple-element.13.refs_0_, bf16[128,4096]{1,0:T(8,128)(2,1)S(1)} %collective-permute-done.refs_1_.earlier_ref, bf16[16384,128]{1,0:T(8,128)(2,1)} %get-tuple-element.14.refs_2_), custom_call_target="tpu_custom_call" | custom-call | tf_op jit(solution)/shard_map/fwd_across/pallas_call | solution.py:128
  165.4 7.7 %bwd_across.1 = bf16[128,4096]{1,0:T(8,128)(2,1)} custom-call(f32[128,4096]{1,0:T(8,128)S(1)} %copy-done.3, bf16[128,4096]{1,0:T(8,128)(2,1)} %collective-permute-done.1.refs_1_, bf16[16384,128]{1,0:T(8,128)(2,1)} %get-tuple-element.16.refs_2_), custom_call_target="tpu_custom_call" | custom-call | tf_op jit(solution)/shard_map/bwd_across/pallas_call | solution.py:128
  173.1 0.6 slice_multiply_fusion
  173.7 0.7 div.13
  (15 shorter events, 0.1 us)
Async XLA Ops:
  0.6 57.1 %collective-permute-start = (bf16[128,4096]{1,0:T(8,128)(2,1)}, bf16[128,4096]{1,0:T(8,128)(2,1)S(1)}, u32[]{:S(2)}, u32[]{:S(2)}) collective-permute-start(bf16[128,4096]{1,0:T(8,128)(2,1)} %bitcast.9), channel_id=1, source_target_pairs={{0,1},{1,2},{2,3},{3,4},{4,5},{5,6},{6,7},{7,8},{8,9},{9,10},{10,1... | collective-permute-start | bytes 3145736 | tf_op jit(solution)/shard_map/ppermute | solution.py:204
  4.7 160.8 %collective-permute-start.1 = (bf16[128,4096]{1,0:T(8,128)(2,1)}, bf16[128,4096]{1,0:T(8,128)(2,1)}, u32[]{:S(2)}, u32[]{:S(2)}) collective-permute-start(bf16[128,4096]{1,0:T(8,128)(2,1)} %bitcast.12), channel_id=1, source_target_pairs={{1,0},{2,1},{3,2},{4,3},{5,4},{6,5},{7,6},{8,7},{9,8},{10,9},{11,1... | collective-permute-start | bytes 3145736 | tf_op jit(solution)/shard_map/ppermute | solution.py:205
  6.0 0.8 copy-start.4
  42.7 1.9 %copy-start = (bf16[16384,128]{1,0:T(8,128)(2,1)}, bf16[16384,128]{1,0:T(8,128)(2,1)S(1)}, u32[]{:S(2)}) copy-start(bf16[16384,128]{1,0:T(8,128)(2,1)S(1)} %get-tuple-element.11.fwd_ref) | copy-start | bytes 12582916
  44.7 1.2 copy-start.1
  45.9 1.2 copy-start.2
  47.1 0.7 copy-start.5
  125.7 47.4 %all-to-all-start.1 = ((f32[16,1,72]{2,1,0:T(1,128)}), f32[16,1,72]{2,1,0:T(1,128)S(1)}, u32[]{:S(2)}, u32[]{:S(2)}) async-start(f32[16,1,72]{2,1,0:T(1,128)} %bitcast.8), calls=%async_computation.1 | async-start | bytes 16384 | tf_op jit(solution)/shard_map/all_to_all | solution.py:195
  157.8 7.6 %copy-start.3 = (f32[128,4096]{1,0:T(8,128)S(1)}, f32[128,4096]{1,0:T(8,128)}, u32[]{:S(2)}) copy-start(f32[128,4096]{1,0:T(8,128)} %get-tuple-element.15.refs_0_) | copy-start | bytes 6291460
where the time goes:
time: 175 us; the launch traced here: 174 us
  Pallas kernels  69.6 us (40%)
  blocking collectives  58.2 us (33%)
  starting transfers between devices  37.4 us (21%)
  local copies, waits for them, and re-layouts  7.08 us (4%)
    all_to_all x1, blocking collectives, reduced(): got = jnp.sum(lax.all_to_all(sent, 'ctx', 0, 0, tiled=True), axis=0)  58.2 us
    pallas_call x1, Pallas kernels, toeplitz(): pl.pallas_call(toeplitz_kernel, grid=(groups // step,), in_specs=[pl.Bloc...  35.9 us
    all_to_all x1, starting transfers between devices, reduced(): got = jnp.sum(lax.all_to_all(sent, 'dp', 0, 0, tiled=True), axis=0)  32.1 us
    pallas_call x2, Pallas kernels, across_part(): pl.pallas_call(lambda *refs: across_kernel(window, *refs), grid=(chans //...  15.3 us
    pallas_call x1, Pallas kernels, local_part(): pl.pallas_call(local_kernel, grid=(chans // (TILES * LANES),), in_specs=[...  9.85 us
    pallas_call x1, Pallas kernels, lag_sums(): pl.pallas_call(lag_kernel, grid=(chans // (TILES * LANES),), in_specs=[ch...  8.49 us
    unnamed x12, local copies, waits for them, and re-layouts  5.94 us
    ppermute x1, starting transfers between devices, shards(): earlier = lax.ppermute(cur, 'ctx', [(i, i + 1) for i in range(ctx - 1)])  4.01 us
  transfers between devices with their start and end apart: 3, of which 0 were waited for; matrix products, arithmetic and copies ran while one was open for 1% of the time, Pallas kernels for 40%

commit v1 on v0

v1 whole, which is shorter than its diff:
```python
import functools
import math

import jax
import jax.numpy as jnp
from jax import lax
from jax.experimental import pallas as pl
from jax.experimental.pallas import tpu as pltpu
from jax.sharding import PartitionSpec as P

CH = 16
TAPS = 128
LANES = 128
PER = LANES // CH
HALF = 64
QUARTER = 32
TILES = 8
WIDE = TILES * LANES
ROW = 4
VMEM = 60 * 1024 * 1024
SHORT = pl.CostEstimate(flops=1, bytes_accessed=1, transcendentals=0)


def params():
    return pltpu.CompilerParams(vmem_limit_bytes=VMEM)


def circulant_kernel(taps_ref, out_ref):
    taps = taps_ref[...]
    groups = taps.shape[0]
    source = lax.broadcasted_iota(jnp.int32, (TAPS, TAPS), 0)
    target = lax.broadcasted_iota(jnp.int32, (TAPS, TAPS), 1)
    turn = jnp.where((source + target) % TAPS == 0, 1.0, 0.0).astype(jnp.bfloat16)
    back = jnp.dot(taps, turn, preferred_element_type=jnp.float32)
    for way, rows in enumerate((back, taps.astype(jnp.float32))):
        first = [
            pltpu.roll(jnp.broadcast_to(rows[g : g + 1], (8, TAPS)), 0, 1, stride=1, stride_axis=0)
            for g in range(groups)
        ]
        first = jnp.concatenate(first, axis=0)
        for pair in range(HALF // 16):
            low = pltpu.roll(first, pair * 16, 1) if pair else first
            high = pltpu.roll(first, pair * 16 + 8, 1)
            both = jnp.concatenate([low.reshape(groups, 8, TAPS), high.reshape(groups, 8, TAPS)], axis=1)
            out_ref[way, :, pair * 16 : pair * 16 + 16, :] = both.astype(jnp.bfloat16)


def circulants(filters):
    groups = filters.shape[0]
    step = 64
    out = pl.pallas_call(
        circulant_kernel,
        grid=(groups // step,),
        in_specs=[pl.BlockSpec((step, TAPS), lambda i: (i, 0))],
        out_specs=pl.BlockSpec((2, step, HALF, TAPS), lambda i: (0, i, 0, 0)),
        out_shape=jax.ShapeDtypeStruct((2, groups, HALF, TAPS), jnp.bfloat16),
        compiler_params=params(),
        cost_estimate=SHORT,
        name="circulants",
    )(filters)
    return out.reshape(2, groups * HALF, TAPS)


def inside_mask(forward):
    row = lax.broadcasted_iota(jnp.int32, (PER * HALF, TAPS), 0) % HALF
    lane = lax.broadcasted_iota(jnp.int32, (PER * HALF, TAPS), 1)
    kept = (lane <= row) | (lane >= HALF) if forward else lane >= row
    return jnp.where(kept, 1.0, 0.0).astype(jnp.bfloat16)


def picked(product):
    lane = lax.broadcasted_iota(jnp.int32, (HALF, 2 * LANES), 1)
    owner = (lane % LANES) // CH
    kept = product[:HALF]
    for group in range(1, PER):
        kept = jnp.where(owner == group, product[group * HALF : (group + 1) * HALF], kept)
    return jnp.concatenate([kept[:, :LANES], kept[:, LANES:]], axis=0)


def convolved(forward, matrix, mask, own, halo, skip):
    inside = matrix * mask
    both = jnp.concatenate([inside, matrix - inside], axis=1)
    none = jnp.zeros_like(own[:HALF])
    if forward:
        left = [own[:HALF], halo[HALF:], halo[:HALF], none]
        right = [own[HALF:], own[:HALF], halo[HALF:], none]
    else:
        left = [own, halo[:HALF], none]
        right = [own[HALF:], halo[:HALF], halo[HALF:], none]
    window = jnp.concatenate([jnp.concatenate(left, axis=0), jnp.concatenate(right, axis=0)], axis=1)
    total = picked(jnp.dot(both, window, preferred_element_type=jnp.float32))
    return (total + skip * own.astype(jnp.float32)).astype(jnp.bfloat16)


def cross_sums(earlier, cur, grad):
    both = jnp.concatenate([earlier, cur], axis=0)
    span = QUARTER + TAPS
    blocks = TAPS // QUARTER
    values = jnp.concatenate([both[b * QUARTER : b * QUARTER + span] for b in range(blocks)], axis=1)
    grads = jnp.concatenate([grad[b * QUARTER : (b + 1) * QUARTER] for b in range(blocks)], axis=1)
    lane = lax.broadcasted_iota(jnp.int32, grads.shape, 1)
    owner = (lane % LANES) // CH
    zero = jnp.zeros_like(grads)
    masked = jnp.concatenate([jnp.where(owner == group, grads, zero) for group in range(PER)], axis=0)
    cross = lax.dot_general(masked, values, (((1,), (1,)), ((), ())), preferred_element_type=jnp.float32)
    cross = jnp.concatenate([cross, jnp.zeros((cross.shape[0], 2 * TAPS - span), jnp.float32)], axis=1)
    rows = 8
    parts = cross.reshape(PER, QUARTER // rows, rows, 2 * TAPS)
    total = parts[:, 0].reshape(PER * rows, 2 * TAPS)
    for part in range(1, QUARTER // rows):
        moved = pltpu.roll(parts[:, part].reshape(PER * rows, 2 * TAPS), 2 * TAPS - part * rows, 1)
        total = total + moved
    row = lax.broadcasted_iota(jnp.int32, total.shape, 0) % rows
    for bit in (1, 2, 4):
        total = jnp.where(row & bit != 0, pltpu.roll(total, 2 * TAPS - bit, 1), total)
    return jnp.sum(total.reshape(PER, rows, 2 * TAPS), axis=1)


def by_lag(sums):
    source = lax.broadcasted_iota(jnp.int32, (2 * TAPS, TAPS), 0)
    target = lax.broadcasted_iota(jnp.int32, (2 * TAPS, TAPS), 1)
    turn = jnp.where(source + target == TAPS, 1.0, 0.0)
    return jnp.dot(sums, turn, precision=lax.Precision.HIGHEST, preferred_element_type=jnp.float32)


def tile_of(index):
    return slice(index * LANES, (index + 1) * LANES), slice(index * PER * HALF, (index + 1) * PER * HALF)


def main_kernel(place_ref, earlier_ref, cur_ref, grad_ref, later_ref, fwd_ref, bwd_ref, skip_ref, conv_ref, back_ref, lag_ref, diag_ref):
    for at_end, forward, own_ref, halo_ref, matrix_ref, out_ref in (
        (0, True, cur_ref, earlier_ref, fwd_ref, conv_ref),
        (ROW - 1, False, grad_ref, later_ref, bwd_ref, back_ref),
    ):

        @pl.when(place_ref[0] != at_end)
        def _():
            mask = inside_mask(forward)
            for index in range(TILES):
                lanes, rows = tile_of(index)
                own, halo = own_ref[:, lanes], halo_ref[:, lanes]
                out_ref[:, lanes] = convolved(forward, matrix_ref[0, rows], mask, own, halo, skip_ref[:, lanes])

    sums = []
    for index in range(TILES):
        lanes, _ = tile_of(index)
        earlier, cur, grad = (ref[:, lanes] for ref in (earlier_ref, cur_ref, grad_ref))
        diag_ref[:, lanes] = jnp.sum(cur.astype(jnp.float32) * grad.astype(jnp.float32), axis=0, keepdims=True)
        sums.append(cross_sums(earlier, cur, grad))
    lag_ref[...] = by_lag(jnp.concatenate(sums, axis=0))


def main_part(place, earlier, cur, grad, later, matrices, skip):
    tokens, chans = cur.shape
    spec = pl.BlockSpec((tokens, WIDE), lambda i, place: (0, i))
    row_spec = pl.BlockSpec((1, WIDE), lambda i, place: (0, i))
    narrow = jax.ShapeDtypeStruct((tokens, chans), jnp.bfloat16)
    return pl.pallas_call(
        main_kernel,
        grid_spec=pltpu.PrefetchScalarGridSpec(
            num_scalar_prefetch=1,
            grid=(chans // WIDE,),
            in_specs=[spec] * 4
            + [
                pl.BlockSpec((1, TILES * PER * HALF, TAPS), lambda i, place: (0, i, 0)),
                pl.BlockSpec((1, TILES * PER * HALF, TAPS), lambda i, place: (1, i, 0)),
                row_spec,
            ],
            out_specs=[spec, spec, pl.BlockSpec((TILES * PER, TAPS), lambda i, place: (i, 0)), row_spec],
        ),
        out_shape=[
            narrow,
            narrow,
            jax.ShapeDtypeStruct((chans // CH, TAPS), jnp.float32),
            jax.ShapeDtypeStruct((1, chans), jnp.float32),
        ],
        compiler_params=params(),
        cost_estimate=SHORT,
        name="main_part",
    )(place, earlier, cur, grad, later, matrices, matrices, skip)


def far_lag_kernel(place_ref, halo_ref, cur_ref, grad_ref, lag_ref, out_ref):
    place = place_ref[0]

    def added(earlier_ref, own_ref):
        sums = []
        for index in range(TILES):
            lanes, _ = tile_of(index)
            earlier = earlier_ref[:, lanes]
            sums.append(cross_sums(earlier, jnp.zeros_like(earlier), own_ref[:, lanes]))
        out_ref[...] = lag_ref[...] + by_lag(jnp.concatenate(sums, axis=0))

    @pl.when(place == 0)
    def _():
        added(halo_ref, grad_ref)

    @pl.when(place == ROW - 1)
    def _():
        added(cur_ref, halo_ref)

    @pl.when((place != 0) & (place != ROW - 1))
    def _():
        out_ref[...] = lag_ref[...]


def far_lag(place, halo, cur, grad, lagged):
    tokens, chans = cur.shape
    steps = chans // WIDE // 2
    lag_spec = pl.BlockSpec((TILES * PER, TAPS), lambda i, place: (jnp.where(place[0] == ROW - 1, steps, 0) + i, 0))
    return pl.pallas_call(
        far_lag_kernel,
        grid_spec=pltpu.PrefetchScalarGridSpec(
            num_scalar_prefetch=1,
            grid=(steps,),
            in_specs=[
                pl.BlockSpec((tokens, WIDE), lambda i, place: (0, i)),
                pl.BlockSpec((tokens, WIDE), lambda i, place: (0, steps + i)),
                pl.BlockSpec((tokens, WIDE), lambda i, place: (0, i)),
                lag_spec,
            ],
            out_specs=lag_spec,
        ),
        out_shape=jax.ShapeDtypeStruct(lagged.shape, jnp.float32),
        input_output_aliases={4: 0},
        compiler_params=params(),
        cost_estimate=SHORT,
        name="far_lag",
    )(place, halo, cur, grad, lagged)


def far_fix_kernel(place_ref, halo_ref, cur_ref, grad_ref, matrix_ref, fwd_skip_ref, bwd_skip_ref, conv_ref, back_ref, conv_out_ref, back_out_ref):
    def redo(forward, own_ref, skip_ref, out_ref):
        mask = inside_mask(forward)
        for index in range(TILES):
            lanes, rows = tile_of(index)
            own, halo = own_ref[:, lanes], halo_ref[:, lanes]
            out_ref[:, lanes] = convolved(forward, matrix_ref[0, rows], mask, own, halo, skip_ref[:, lanes])

    @pl.when(place_ref[0] == 0)
    def _():
        redo(True, cur_ref, fwd_skip_ref, conv_out_ref)

    @pl.when(place_ref[0] != 0)
    def _():
        conv_out_ref[...] = conv_ref[...]

    @pl.when(place_ref[0] == ROW - 1)
    def _():
        redo(False, grad_ref, bwd_skip_ref, back_out_ref)

    @pl.when(place_ref[0] != ROW - 1)
    def _():
        back_out_ref[...] = back_ref[...]


def far_fix(phase, place, halo, cur, grad, matrices, skip, conv, back):
    tokens, chans = cur.shape
    steps = chans // WIDE // 2
    fwd_at, bwd_at = (0, steps) if phase == 0 else (steps, 0)
    fwd_spec = pl.BlockSpec((tokens, WIDE), lambda i, place: (0, fwd_at + i))
    bwd_spec = pl.BlockSpec((tokens, WIDE), lambda i, place: (0, bwd_at + i))

    def matrix_at(i, place):
        last = place[0] == ROW - 1
        return (jnp.where(last, 1, 0), jnp.where(last, bwd_at, fwd_at) + i, 0)

    return pl.pallas_call(
        far_fix_kernel,
        grid_spec=pltpu.PrefetchScalarGridSpec(
            num_scalar_prefetch=1,
            grid=(steps,),
            in_specs=[
                pl.BlockSpec((tokens, WIDE), lambda i, place: (0, i)),
                fwd_spec,
                bwd_spec,
                pl.BlockSpec((1, TILES * PER * HALF, TAPS), matrix_at),
                pl.BlockSpec((1, WIDE), lambda i, place: (0, fwd_at + i)),
                pl.BlockSpec((1, WIDE), lambda i, place: (0, bwd_at + i)),
                fwd_spec,
                bwd_spec,
            ],
            out_specs=[fwd_spec, bwd_spec],
        ),
        out_shape=[jax.ShapeDtypeStruct((tokens, chans), jnp.bfloat16)] * 2,
        input_output_aliases={7: 0, 8: 1},
        compiler_params=params(),
        cost_estimate=SHORT,
        name=("early_fix", "late_fix")[phase],
    )(place, halo, cur, grad, matrices, skip, skip, conv, back)


def over_plane(lagged, diagonal):
    ctx, dp = lax.axis_size("ctx"), lax.axis_size("dp")
    pairs = [[y * 2 * ROW + z * ROW + x for y in range(ctx // ROW // 2) for x in range(ROW)] for z in range(2)]
    sent = jnp.concatenate([lagged.reshape(ctx, -1), diagonal.reshape(ctx, -1)], axis=1)
    sent = sent.reshape(-1, 2, ROW, sent.shape[1]).transpose(0, 2, 1, 3).reshape(ctx // 2, -1)
    got = jnp.sum(lax.all_to_all(sent, "ctx", 0, 0, axis_index_groups=pairs, tiled=True), axis=0).reshape(2, -1)
    groups = lagged.shape[0] // ctx
    taps = got[:, : groups * TAPS].reshape(2, groups, dp, TAPS // dp).transpose(0, 2, 1, 3).reshape(2 * dp, -1)
    return jnp.concatenate([taps, got[:, groups * TAPS :].reshape(2 * dp, -1)], axis=1)


def over_column(sent):
    ctx, dp = lax.axis_size("ctx"), lax.axis_size("dp")
    columns = [
        [d * ctx + y * 2 * ROW + z * ROW + x for z in range(2) for d in range(dp)]
        for y in range(ctx // ROW // 2)
        for x in range(ROW)
    ]
    return jnp.sum(lax.all_to_all(sent, ("dp", "ctx"), 0, 0, axis_index_groups=columns, tiled=True), axis=0)


def in_order(step, *arrays):
    there = lax.axis_index("ctx") < lax.axis_size("ctx")
    shapes = jax.eval_shape(step, *arrays)
    nothing = lambda *_: jax.tree.map(lambda shape: jnp.zeros(shape.shape, shape.dtype), shapes)
    return lax.cond(there, step, nothing, *arrays)


def permuted(array, pairs):
    return lax.ppermute(array, "ctx", pairs)


def shards(features, cotangent, filters, skip_gain):
    ctx = lax.axis_size("ctx")
    token_total = lax.axis_size("dp") * features.shape[0] * features.shape[1] * ctx
    cur, grad = features[0], cotangent[0]
    skip = skip_gain.reshape(1, -1)
    half = cur.shape[1] // 2
    x = lax.axis_index("ctx") % ROW
    place = x.astype(jnp.int32).reshape(1)
    near = [i for i in range(ctx - 1) if i % ROW != ROW - 1]
    far = [i for i in range(ctx - 1) if i % ROW == ROW - 1]
    straight = [(i, i + 1) for i in far] + [(i + 1, i) for i in far]
    aside = [(i, i - 1) for i in far] + [(i + 1, i + 2) for i in far]
    onward = [(i - 1, i + 2) for i in far] + [(i + 2, i - 1) for i in far]
    home = [(i + 2, i + 1) for i in far] + [(i - 1, i) for i in far]

    last = x == ROW - 1
    early = permuted(jnp.where(last, cur[:, :half], grad[:, half:]), straight)
    late = permuted(jnp.where(last, cur[:, half:], grad[:, :half]), aside)
    earlier = permuted(cur, [(i, i + 1) for i in near])
    later = permuted(grad, [(i + 1, i) for i in near])
    matrices = circulants(filters)
    earlier, late, matrices = lax.optimization_barrier((earlier, late, matrices))
    late = permuted(late, onward)
    conv, back, lagged, diagonal = main_part(place, earlier, cur, grad, later, matrices, skip)
    early, lagged = lax.optimization_barrier((early, lagged))
    lagged = far_lag(place, early, cur, grad, lagged)
    conv, back = far_fix(0, place, early, cur, grad, matrices, skip, conv, back)
    lagged, conv, back = lax.optimization_barrier((lagged, conv, back))
    sent = in_order(over_plane, lagged, diagonal)
    late, sent = lax.optimization_barrier((late, sent))
    late = permuted(late, home)
    sums = in_order(over_column, sent)
    conv, back = far_fix(1, place, late, cur, grad, matrices, skip, conv, back)
    cut = sums.shape[0] - cur.shape[1] // (ctx * lax.axis_size("dp"))
    grad_filters = sums[:cut].reshape(-1, TAPS // lax.axis_size("dp")) / math.sqrt(token_total * CH)
    grad_skip = sums[cut:] / math.sqrt(token_total)
    return (conv[None], back[None], grad_filters, grad_skip)


def solution(mesh):
    return jax.shard_map(
        shards,
        mesh=mesh,
        in_specs=(P("dp", "ctx", None), P("dp", "ctx", None), P(), P()),
        out_specs=(P("dp", "ctx", None), P("dp", "ctx", None), P("ctx", "dp"), P(("ctx", "dp"))),
        check_vma=False,
    )
```

time: 175 us -> 136 us (0.78)
  the two profiles are of different devices: /device:TPU:1 before, /device:TPU:2 now
where the time goes in v1:
time: 136 us
  blocking collectives  77.2 us (57%)
  Pallas kernels  28 us (21%)
  starting transfers between devices  13.5 us (10%)
  waiting for transfers between devices  9.75 us (7%)
  local copies, waits for them, and re-layouts  4.14 us (3%)
  other arithmetic  2.51 us (2%)
    all_to_all x1, blocking collectives, over_plane(): lax.all_to_all(sent, 'ctx', 0, 0, axis_index_groups=pairs, tiled=True)  42.5 us
    all_to_all x1, blocking collectives, over_column(): lax.all_to_all(sent, ('dp', 'ctx'), 0, 0, axis_index_groups=columns, tile...  34.8 us
    pallas_call x1, Pallas kernels, main_part(): pl.pallas_call(main_kernel, grid_spec=pltpu.PrefetchScalarGridSpec(num_sc...  14.3 us
    ppermute x6, starting transfers between devices, permuted(): return lax.ppermute(array, 'ctx', pairs)  13.5 us
    ppermute x6, waiting for transfers between devices, permuted(): return lax.ppermute(array, 'ctx', pairs)  9.75 us
    pallas_call x2, Pallas kernels, far_fix(): pl.pallas_call(far_fix_kernel, grid_spec=pltpu.PrefetchScalarGridSpec(num...  6.4 us
    pallas_call x1, Pallas kernels, circulants(): pl.pallas_call(circulant_kernel, grid=(groups // step,), in_specs=[pl.Blo...  5.95 us
  transfers between devices with their start and end apart: 6, of which 2 were waited for; matrix products, arithmetic and copies ran while one was open for 3% of the time, Pallas kernels for 18%

profile of v1, /device:TPU:2, one launch (start us, length us, event | category | flops | bytes accessed | tf_op | source)
XLA Modules:
  0.0 135.8 jit_solution(1518432365954434874)
XLA Ops:
  0.6 3.4 %collective-permute-start = (bf16[128,4096]{1,0:T(8,128)(2,1)}, bf16[128,4096]{1,0:T(8,128)(2,1)S(1)}, u32[]{:S(2)}, u32[]{:S(2)}) collective-permute-start(bf16[128,4096]{1,0:T(8,128)(2,1)} %bitcast.24), channel_id=1, source_target_pairs={{0,1},{1,2},{2,3},{4,5},{5,6},{6,7},{8,9},{9,10},{10,11},{12,13},{... | collective-permute-start | bytes 3145736 | tf_op jit(solution)/shard_map/ppermute | solution.py:322
  4.0 5.8 %collective-permute-start.4 = (bf16[128,4096]{1,0:T(8,128)(2,1)}, bf16[128,4096]{1,0:T(8,128)(2,1)S(1)}, u32[]{:S(2)}, u32[]{:S(2)}) collective-permute-start(bf16[128,4096]{1,0:T(8,128)(2,1)} %bitcast.18), channel_id=1, source_target_pairs={{1,0},{2,1},{3,2},{5,4},{6,5},{7,6},{9,8},{10,9},{11,10},{13,12},{... | collective-permute-start | bytes 3145736 | tf_op jit(solution)/shard_map/ppermute | solution.py:322
  9.8 1.6 %slice_select_fusion = (bf16[128,2048]{1,0:T(8,128)(2,1)S(1)}, bf16[128,2048]{1,0:T(8,128)(2,1)S(1)}) fusion(bf16[128,4096]{1,0:T(8,128)(2,1)} %bitcast.19, bf16[128,4096]{1,0:T(8,128)(2,1)} %bitcast.25, pred[]{:T(512)S(6)} %eq.5), kind=kLoop, calls=%fused_computation.2 | loop fusion | flops 524288 | bytes 3145729 | tf_op jit(solution)/shard_map/jit(_where)/select_n | solution.py:341
  11.5 1.5 %collective-permute-start.1 = (bf16[128,2048]{1,0:T(8,128)(2,1)S(1)}, bf16[128,2048]{1,0:T(8,128)(2,1)}, u32[]{:S(2)}, u32[]{:S(2)}) collective-permute-start(bf16[128,2048]{1,0:T(8,128)(2,1)S(1)} %get-tuple-element.54), channel_id=1, source_target_pairs={{3,2},{7,6},{11,10},{15,14},{19,18},{23,22},{27,26},{4,5},{8,9},{1... | collective-permute-start | bytes 1572872 | tf_op jit(solution)/shard_map/ppermute | solution.py:322
  12.9 0.7 collective-permute-start.3
  13.6 6.0 %circulants.1 = bf16[2,256,64,128]{3,2,1,0:T(8,128)(2,1)} custom-call(bf16[256,128]{1,0:T(8,128)(2,1)} %taps_ref.1), custom_call_target="tpu_custom_call" | custom-call | flops 1 | bytes 1 | tf_op jit(solution)/shard_map/circulants/pallas_call | solution.py:51
  19.6 8.1 %collective-permute-done.earlier_ref = bf16[128,4096]{1,0:T(8,128)(2,1)S(1)} collective-permute-done((bf16[128,4096]{1,0:T(8,128)(2,1)}, bf16[128,4096]{1,0:T(8,128)(2,1)S(1)}, u32[]{:S(2)}, u32[]{:S(2)}) %collective-permute-start) | collective-permute-done | bytes 1048608 | tf_op jit(solution)/shard_map/ppermute | solution.py:322
  27.6 1.4 %collective-permute-start.2 = (bf16[128,2048]{1,0:T(8,128)(2,1)}, bf16[128,2048]{1,0:T(8,128)(2,1)}, u32[]{:S(2)}, u32[]{:S(2)}) collective-permute-start(bf16[128,2048]{1,0:T(8,128)(2,1)} %collective-permute-done.1), channel_id=1, source_target_pairs={{2,5},{6,9},{10,13},{14,17},{18,21},{22,25},{26,29},{5,2},{9,6},{1... | collective-permute-start | bytes 1572872 | tf_op jit(solution)/shard_map/ppermute | solution.py:322
  29.1 1.7 %collective-permute-done.4.later_ref = bf16[128,4096]{1,0:T(8,128)(2,1)S(1)} collective-permute-done((bf16[128,4096]{1,0:T(8,128)(2,1)}, bf16[128,4096]{1,0:T(8,128)(2,1)S(1)}, u32[]{:S(2)}, u32[]{:S(2)}) %collective-permute-start.4) | collective-permute-done | bytes 1048608 | tf_op jit(solution)/shard_map/ppermute | solution.py:322
  30.8 0.9 copy-done.2
  31.7 14.3 %main_part.1 = (bf16[128,4096]{1,0:T(8,128)(2,1)}, bf16[128,4096]{1,0:T(8,128)(2,1)}, f32[256,128]{1,0:T(8,128)S(1)}, f32[1,4096]{1,0:T(1,128)S(1)}) custom-call(s32[1]{0:T(128)} %bitcast.4.place_ref, bf16[128,4096]{1,0:T(8,128)(2,1)} %copy-done.1, bf16[128,4096]{1,0:T(8,128)(2,1)} %bitcast.26, bf16[128,4096]{1,0:T(8,128)(2,1)} %bitcast.20, ...), custom_call_target="tpu_custom_call" | custom-call | flops 1 | bytes 1 | tf_op jit(solution)/shard_map/main_part/pallas_call | solution.py:158
  46.0 0.8 copy-done
  46.8 1.4 far_lag.1
  48.2 3.2 %early_fix.1 = (bf16[128,4096]{1,0:T(8,128)(2,1)}, bf16[128,4096]{1,0:T(8,128)(2,1)}) custom-call(s32[1]{0:T(128)} %bitcast.4.place_ref, bf16[128,2048]{1,0:T(8,128)(2,1)} %copy-done, bf16[128,4096]{1,0:T(8,128)(2,1)} %bitcast.28, bf16[128,4096]{1,0:T(8,128)(2,1)} %bitcast.22, ...), custom_call_target="tpu_custom_call", output_to_operand_aliasing={{0}: (7, {}), {1}: (8, {})} | custom-call | flops 1 | bytes 1 | tf_op jit(solution)/shard_map/early_fix/pallas_call | solution.py:268
  51.4 43.6 %conditional.2 = (f32[32,72]{1,0:T(8,128)S(1)}) conditional(s32[]{:T(128)} %convert_element_type.4, () %tuple.25, (f32[256,128]{1,0:T(8,128)S(1)}, f32[1,4096]{1,0:T(1,128)S(1)}) %tuple.28), branch_computations={%region_0.1_spmd, %region_1.3_spmd} | conditional | flops 73728 | bytes 1721356 | solution.py:318
  51.6 0.2 all_to_all.12
  51.9 42.5 %all_to_all.15 = f32[16,1,2304]{2,1,0:T(1,128)S(1)} all-to-all(f32[16,1,2304]{2,1,0:T(1,128)S(1)} %all_to_all.12), channel_id=1, replica_groups={{0,1,2,3,8,9,10,11,16,17,18,19,24,25,26,27},{4,5,6,7,12,13,14,15,20,21,..., dimensions={0} | all-to-all | bytes 294912 | tf_op jit(solution)/shard_map/cond/branch_1_fun/all_to_all | solution.py:298
  95.0 0.7 collective-permute-start.5
  95.7 34.8 %conditional.3 = (f32[72]{0:T(128)S(1)}) conditional(s32[]{:T(128)} %convert_element_type.4, () %tuple.30, f32[32,72]{1,0:T(8,128)S(1)} %get-tuple-element.55), branch_computations={%region_3.4_spmd, %region_4.6_spmd} | conditional | flops 2232 | bytes 27948 | solution.py:318
  95.7 34.8 %all_to_all.16 = f32[32,1,72]{2,1,0:T(1,128)S(1)} all-to-all(f32[32,1,72]{2,1,0:T(1,128)S(1)} %bitcast.38), channel_id=1, replica_groups={{0,32,64,96,128,160,192,224,256,288,320,352,384,416,448,480,4,36,68,100..., dimensions={0} | all-to-all | bytes 18432 | tf_op jit(solution)/shard_map/cond/branch_1_fun/all_to_all | solution.py:311
  130.6 0.7 div.13
  131.2 0.6 slice_multiply_fusion
  131.8 0.8 copy-done.3
  132.6 3.2 %late_fix.1 = (bf16[128,4096]{1,0:T(8,128)(2,1)}, bf16[128,4096]{1,0:T(8,128)(2,1)}) custom-call(s32[1]{0:T(128)} %bitcast.4.place_ref, bf16[128,2048]{1,0:T(8,128)(2,1)} %copy-done.3, bf16[128,4096]{1,0:T(8,128)(2,1)} %bitcast.29, bf16[128,4096]{1,0:T(8,128)(2,1)} %bitcast.23, ...), custom_call_target="tpu_custom_call", output_to_operand_aliasing={{0}: (7, {}), {1}: (8, {})} | custom-call | flops 1 | bytes 1 | tf_op jit(solution)/shard_map/late_fix/pallas_call | solution.py:268
  (25 shorter events, 1.0 us)
Async XLA Ops:
  0.6 27.0 %collective-permute-start = (bf16[128,4096]{1,0:T(8,128)(2,1)}, bf16[128,4096]{1,0:T(8,128)(2,1)S(1)}, u32[]{:S(2)}, u32[]{:S(2)}) collective-permute-start(bf16[128,4096]{1,0:T(8,128)(2,1)} %bitcast.24), channel_id=1, source_target_pairs={{0,1},{1,2},{2,3},{4,5},{5,6},{6,7},{8,9},{9,10},{10,11},{12,13},{... | collective-permute-start | bytes 3145736 | tf_op jit(solution)/shard_map/ppermute | solution.py:322
  4.0 26.7 %collective-permute-start.4 = (bf16[128,4096]{1,0:T(8,128)(2,1)}, bf16[128,4096]{1,0:T(8,128)(2,1)S(1)}, u32[]{:S(2)}, u32[]{:S(2)}) collective-permute-start(bf16[128,4096]{1,0:T(8,128)(2,1)} %bitcast.18), channel_id=1, source_target_pairs={{1,0},{2,1},{3,2},{5,4},{6,5},{7,6},{9,8},{10,9},{11,10},{13,12},{... | collective-permute-start | bytes 3145736 | tf_op jit(solution)/shard_map/ppermute | solution.py:322
  11.5 8.1 %collective-permute-start.1 = (bf16[128,2048]{1,0:T(8,128)(2,1)S(1)}, bf16[128,2048]{1,0:T(8,128)(2,1)}, u32[]{:S(2)}, u32[]{:S(2)}) collective-permute-start(bf16[128,2048]{1,0:T(8,128)(2,1)S(1)} %get-tuple-element.54), channel_id=1, source_target_pairs={{3,2},{7,6},{11,10},{15,14},{19,18},{23,22},{27,26},{4,5},{8,9},{1... | collective-permute-start | bytes 1572872 | tf_op jit(solution)/shard_map/ppermute | solution.py:322
  12.9 33.1 %collective-permute-start.3 = (bf16[128,2048]{1,0:T(8,128)(2,1)S(1)}, bf16[128,2048]{1,0:T(8,128)(2,1)S(1)}, u32[]{:S(2)}, u32[]{:S(2)}) collective-permute-start(bf16[128,2048]{1,0:T(8,128)(2,1)S(1)} %get-tuple-element.53), channel_id=1, source_target_pairs={{3,4},{7,8},{11,12},{15,16},{19,20},{23,24},{27,28},{4,3},{8,7},{1... | collective-permute-start | bytes 1572872 | tf_op jit(solution)/shard_map/ppermute | solution.py:322
  27.6 3.1 %copy-start.1 = (bf16[128,4096]{1,0:T(8,128)(2,1)}, bf16[128,4096]{1,0:T(8,128)(2,1)S(1)}, u32[]{:S(2)}) copy-start(bf16[128,4096]{1,0:T(8,128)(2,1)S(1)} %collective-permute-done.earlier_ref) | copy-start | bytes 3145732
  27.6 67.4 %collective-permute-start.2 = (bf16[128,2048]{1,0:T(8,128)(2,1)}, bf16[128,2048]{1,0:T(8,128)(2,1)}, u32[]{:S(2)}, u32[]{:S(2)}) collective-permute-start(bf16[128,2048]{1,0:T(8,128)(2,1)} %collective-permute-done.1), channel_id=1, source_target_pairs={{2,5},{6,9},{10,13},{14,17},{18,21},{22,25},{26,29},{5,2},{9,6},{1... | collective-permute-start | bytes 1572872 | tf_op jit(solution)/shard_map/ppermute | solution.py:322
  30.8 1.0 copy-start.2
  46.0 0.8 copy-start
  95.0 36.8 %collective-permute-start.5 = (bf16[128,2048]{1,0:T(8,128)(2,1)}, bf16[128,2048]{1,0:T(8,128)(2,1)S(1)}, u32[]{:S(2)}, u32[]{:S(2)}) collective-permute-start(bf16[128,2048]{1,0:T(8,128)(2,1)} %collective-permute-done.2), channel_id=1, source_target_pairs={{5,4},{9,8},{13,12},{17,16},{21,20},{25,24},{29,28},{2,3},{6,7},{1... | collective-permute-start | bytes 1572872 | tf_op jit(solution)/shard_map/ppermute | solution.py:322
  131.8 0.8 copy-start.3

commit v2 on v1

--- a/solution.py
+++ b/solution.py
@@ -16,13 +16,15 @@
 QUARTER = 32
 TILES = 8
 WIDE = TILES * LANES
+MAIN_TILES = 16
+MAIN_WIDE = MAIN_TILES * LANES
 ROW = 4
-VMEM = 60 * 1024 * 1024
+LARGE, SMALL = 56 * 1024 * 1024, 24 * 1024 * 1024
 SHORT = pl.CostEstimate(flops=1, bytes_accessed=1, transcendentals=0)
 
 
-def params():
-    return pltpu.CompilerParams(vmem_limit_bytes=VMEM)
+def params(limit=SMALL):
+    return pltpu.CompilerParams(vmem_limit_bytes=limit)
 
 
 def circulant_kernel(taps_ref, out_ref):
@@ -103,23 +105,24 @@
     zero = jnp.zeros_like(grads)
     masked = jnp.concatenate([jnp.where(owner == group, grads, zero) for group in range(PER)], axis=0)
     cross = lax.dot_general(masked, values, (((1,), (1,)), ((), ())), preferred_element_type=jnp.float32)
-    cross = jnp.concatenate([cross, jnp.zeros((cross.shape[0], 2 * TAPS - span), jnp.float32)], axis=1)
+    rest = jnp.concatenate([cross[:, TAPS:], jnp.zeros((cross.shape[0], 2 * TAPS - span), jnp.float32)], axis=1)
+    row = lax.broadcasted_iota(jnp.int32, rest.shape, 0) % QUARTER
+    folded = jnp.where(lax.broadcasted_iota(jnp.int32, rest.shape, 1) > row, cross[:, :TAPS], rest)
     rows = 8
-    parts = cross.reshape(PER, QUARTER // rows, rows, 2 * TAPS)
-    total = parts[:, 0].reshape(PER * rows, 2 * TAPS)
+    parts = folded.reshape(PER, QUARTER // rows, rows, TAPS)
+    total = parts[:, 0].reshape(PER * rows, TAPS)
     for part in range(1, QUARTER // rows):
-        moved = pltpu.roll(parts[:, part].reshape(PER * rows, 2 * TAPS), 2 * TAPS - part * rows, 1)
-        total = total + moved
+        total = total + pltpu.roll(parts[:, part].reshape(PER * rows, TAPS), TAPS - part * rows, 1)
     row = lax.broadcasted_iota(jnp.int32, total.shape, 0) % rows
     for bit in (1, 2, 4):
-        total = jnp.where(row & bit != 0, pltpu.roll(total, 2 * TAPS - bit, 1), total)
-    return jnp.sum(total.reshape(PER, rows, 2 * TAPS), axis=1)
+        total = jnp.where(row & bit != 0, pltpu.roll(total, TAPS - bit, 1), total)
+    return jnp.sum(total.reshape(PER, rows, TAPS), axis=1)
 
 
 def by_lag(sums):
-    source = lax.broadcasted_iota(jnp.int32, (2 * TAPS, TAPS), 0)
-    target = lax.broadcasted_iota(jnp.int32, (2 * TAPS, TAPS), 1)
-    turn = jnp.where(source + target == TAPS, 1.0, 0.0)
+    source = lax.broadcasted_iota(jnp.int32, (TAPS, TAPS), 0)
+    target = lax.broadcasted_iota(jnp.int32, (TAPS, TAPS), 1)
+    turn = jnp.where((source + target) % TAPS == 0, 1.0, 0.0)
     return jnp.dot(sums, turn, precision=lax.Precision.HIGHEST, preferred_element_type=jnp.float32)
 
 
@@ -136,13 +139,13 @@
         @pl.when(place_ref[0] != at_end)
         def _():
             mask = inside_mask(forward)
-            for index in range(TILES):
+            for index in range(MAIN_TILES):
                 lanes, rows = tile_of(index)
                 own, halo = own_ref[:, lanes], halo_ref[:, lanes]
                 out_ref[:, lanes] = convolved(forward, matrix_ref[0, rows], mask, own, halo, skip_ref[:, lanes])
 
     sums = []
-    for index in range(TILES):
+    for index in range(MAIN_TILES):
         lanes, _ = tile_of(index)
         earlier, cur, grad = (ref[:, lanes] for ref in (earlier_ref, cur_ref, grad_ref))
         diag_ref[:, lanes] = jnp.sum(cur.astype(jnp.float32) * grad.astype(jnp.float32), axis=0, keepdims=True)
@@ -152,21 +155,21 @@
 
 def main_part(place, earlier, cur, grad, later, matrices, skip):
     tokens, chans = cur.shape
-    spec = pl.BlockSpec((tokens, WIDE), lambda i, place: (0, i))
-    row_spec = pl.BlockSpec((1, WIDE), lambda i, place: (0, i))
+    spec = pl.BlockSpec((tokens, MAIN_WIDE), lambda i, place: (0, i))
+    row_spec = pl.BlockSpec((1, MAIN_WIDE), lambda i, place: (0, i))
     narrow = jax.ShapeDtypeStruct((tokens, chans), jnp.bfloat16)
     return pl.pallas_call(
         main_kernel,
         grid_spec=pltpu.PrefetchScalarGridSpec(
             num_scalar_prefetch=1,
-            grid=(chans // WIDE,),
+            grid=(chans // MAIN_WIDE,),
             in_specs=[spec] * 4
             + [
-                pl.BlockSpec((1, TILES * PER * HALF, TAPS), lambda i, place: (0, i, 0)),
-                pl.BlockSpec((1, TILES * PER * HALF, TAPS), lambda i, place: (1, i, 0)),
+                pl.BlockSpec((1, MAIN_TILES * PER * HALF, TAPS), lambda i, place: (0, i, 0)),
+                pl.BlockSpec((1, MAIN_TILES * PER * HALF, TAPS), lambda i, place: (1, i, 0)),
                 row_spec,
             ],
-            out_specs=[spec, spec, pl.BlockSpec((TILES * PER, TAPS), lambda i, place: (i, 0)), row_spec],
+            out_specs=[spec, spec, pl.BlockSpec((MAIN_TILES * PER, TAPS), lambda i, place: (i, 0)), row_spec],
         ),
         out_shape=[
             narrow,
@@ -174,13 +177,17 @@
             jax.ShapeDtypeStruct((chans // CH, TAPS), jnp.float32),
             jax.ShapeDtypeStruct((1, chans), jnp.float32),
         ],
-        compiler_params=params(),
+        compiler_params=params(40 * 1024 * 1024),
         cost_estimate=SHORT,
         name="main_part",
     )(place, earlier, cur, grad, later, matrices, matrices, skip)
 
 
-def far_lag_kernel(place_ref, halo_ref, cur_ref, grad_ref, lag_ref, out_ref):
+def far_fix_kernel(place_ref, halo_ref, cur_ref, grad_ref, matrix_ref, fwd_skip_ref, bwd_skip_ref, conv_ref, back_ref, *refs):
+    if len(refs) == 2:
+        conv_out_ref, back_out_ref = refs
+    else:
+        fwd_values_ref, bwd_grads_ref, lag_ref, conv_out_ref, back_out_ref, lag_out_ref = refs
     place = place_ref[0]
 
     def added(earlier_ref, own_ref):
@@ -189,47 +196,8 @@
             lanes, _ = tile_of(index)
             earlier = earlier_ref[:, lanes]
             sums.append(cross_sums(earlier, jnp.zeros_like(earlier), own_ref[:, lanes]))
-        out_ref[...] = lag_ref[...] + by_lag(jnp.concatenate(sums, axis=0))
-
-    @pl.when(place == 0)
-    def _():
-        added(halo_ref, grad_ref)
-
-    @pl.when(place == ROW - 1)
-    def _():
-        added(cur_ref, halo_ref)
-
-    @pl.when((place != 0) & (place != ROW - 1))
-    def _():
-        out_ref[...] = lag_ref[...]
-
-
-def far_lag(place, halo, cur, grad, lagged):
-    tokens, chans = cur.shape
-    steps = chans // WIDE // 2
-    lag_spec = pl.BlockSpec((TILES * PER, TAPS), lambda i, place: (jnp.where(place[0] == ROW - 1, steps, 0) + i, 0))
-    return pl.pallas_call(
-        far_lag_kernel,
-        grid_spec=pltpu.PrefetchScalarGridSpec(
-            num_scalar_prefetch=1,
-            grid=(steps,),
-            in_specs=[
-                pl.BlockSpec((tokens, WIDE), lambda i, place: (0, i)),
-                pl.BlockSpec((tokens, WIDE), lambda i, place: (0, steps + i)),
-                pl.BlockSpec((tokens, WIDE), lambda i, place: (0, i)),
-                lag_spec,
-            ],
-            out_specs=lag_spec,
-        ),
-        out_shape=jax.ShapeDtypeStruct(lagged.shape, jnp.float32),
-        input_output_aliases={4: 0},
-        compiler_params=params(),
-        cost_estimate=SHORT,
-        name="far_lag",
-    )(place, halo, cur, grad, lagged)
-
-
-def far_fix_kernel(place_ref, halo_ref, cur_ref, grad_ref, matrix_ref, fwd_skip_ref, bwd_skip_ref, conv_ref, back_ref, conv_out_ref, back_out_ref):
+        lag_out_ref[...] = lag_ref[...] + by_lag(jnp.concatenate(sums, axis=0))
+
     def redo(forward, own_ref, skip_ref, out_ref):
         mask = inside_mask(forward)
         for index in range(TILES):
@@ -237,57 +205,78 @@
             own, halo = own_ref[:, lanes], halo_ref[:, lanes]
             out_ref[:, lanes] = convolved(forward, matrix_ref[0, rows], mask, own, halo, skip_ref[:, lanes])
 
-    @pl.when(place_ref[0] == 0)
+    @pl.when(place == 0)
     def _():
         redo(True, cur_ref, fwd_skip_ref, conv_out_ref)
-
-    @pl.when(place_ref[0] != 0)
+        if len(refs) != 2:
+            added(halo_ref, fwd_values_ref)
+
+    @pl.when(place != 0)
     def _():
         conv_out_ref[...] = conv_ref[...]
 
-    @pl.when(place_ref[0] == ROW - 1)
+    @pl.when(place == ROW - 1)
     def _():
         redo(False, grad_ref, bwd_skip_ref, back_out_ref)
-
-    @pl.when(place_ref[0] != ROW - 1)
+        if len(refs) != 2:
+            added(bwd_grads_ref, halo_ref)
+
+    @pl.when(place != ROW - 1)
     def _():
         back_out_ref[...] = back_ref[...]
 
-
-def far_fix(phase, place, halo, cur, grad, matrices, skip, conv, back):
+    if len(refs) != 2:
+
+        @pl.when((place != 0) & (place != ROW - 1))
+        def _():
+            lag_out_ref[...] = lag_ref[...]
+
+
+def far_fix(place, halo, cur, grad, matrices, skip, conv, back, lagged=None):
     tokens, chans = cur.shape
     steps = chans // WIDE // 2
-    fwd_at, bwd_at = (0, steps) if phase == 0 else (steps, 0)
+    fwd_at, bwd_at = (steps, 0) if lagged is None else (0, steps)
     fwd_spec = pl.BlockSpec((tokens, WIDE), lambda i, place: (0, fwd_at + i))
     bwd_spec = pl.BlockSpec((tokens, WIDE), lambda i, place: (0, bwd_at + i))
 
-    def matrix_at(i, place):
-        last = place[0] == ROW - 1
-        return (jnp.where(last, 1, 0), jnp.where(last, bwd_at, fwd_at) + i, 0)
-
+    def part(i, place):
+        return jnp.where(place[0] == ROW - 1, bwd_at, fwd_at) + i
+
+    in_specs = [
+        pl.BlockSpec((tokens, WIDE), lambda i, place: (0, i)),
+        fwd_spec,
+        bwd_spec,
+        pl.BlockSpec(
+            (1, TILES * PER * HALF, TAPS),
+            lambda i, place: (jnp.where(place[0] == ROW - 1, 1, 0), part(i, place), 0),
+        ),
+        pl.BlockSpec((1, WIDE), lambda i, place: (0, fwd_at + i)),
+        pl.BlockSpec((1, WIDE), lambda i, place: (0, bwd_at + i)),
+        fwd_spec,
+        bwd_spec,
+    ]
+    out_specs = [fwd_spec, bwd_spec]
+    out_shape = [jax.ShapeDtypeStruct((tokens, chans), jnp.bfloat16)] * 2
+    aliases = {7: 0, 8: 1}
+    args = [place, halo, cur, grad, matrices, skip, skip, conv, back]
+    if lagged is not None:
+        lag_spec = pl.BlockSpec((TILES * PER, TAPS), lambda i, place: (part(i, place), 0))
+        in_specs += [fwd_spec, bwd_spec, lag_spec]
+        out_specs += [lag_spec]
+        out_shape += [jax.ShapeDtypeStruct(lagged.shape, jnp.float32)]
+        aliases[11] = 2
+        args += [grad, cur, lagged]
     return pl.pallas_call(
         far_fix_kernel,
         grid_spec=pltpu.PrefetchScalarGridSpec(
-            num_scalar_prefetch=1,
-            grid=(steps,),
-            in_specs=[
-                pl.BlockSpec((tokens, WIDE), lambda i, place: (0, i)),
-                fwd_spec,
-                bwd_spec,
-                pl.BlockSpec((1, TILES * PER * HALF, TAPS), matrix_at),
-                pl.BlockSpec((1, WIDE), lambda i, place: (0, fwd_at + i)),
-                pl.BlockSpec((1, WIDE), lambda i, place: (0, bwd_at + i)),
-                fwd_spec,
-                bwd_spec,
-            ],
-            out_specs=[fwd_spec, bwd_spec],
+            num_scalar_prefetch=1, grid=(steps,), in_specs=in_specs, out_specs=out_specs
         ),
-        out_shape=[jax.ShapeDtypeStruct((tokens, chans), jnp.bfloat16)] * 2,
-        input_output_aliases={7: 0, 8: 1},
-        compiler_params=params(),
+        out_shape=out_shape,
+        input_output_aliases=aliases,
+        compiler_params=params(LARGE if lagged is None else SMALL),
         cost_estimate=SHORT,
-        name=("early_fix", "late_fix")[phase],
-    )(place, halo, cur, grad, matrices, skip, skip, conv, back)
+        name="late_fix" if lagged is None else "early_fix",
+    )(*args)
 
 
 def over_plane(lagged, diagonal):
@@ -338,23 +327,23 @@
     home = [(i + 2, i + 1) for i in far] + [(i - 1, i) for i in far]
 
     last = x == ROW - 1
-    early = permuted(jnp.where(last, cur[:, :half], grad[:, half:]), straight)
-    late = permuted(jnp.where(last, cur[:, half:], grad[:, :half]), aside)
+    early = jnp.where(last, cur[:, :half], grad[:, half:])
+    late = jnp.where(last, cur[:, half:], grad[:, :half])
+    early, late, filters = lax.optimization_barrier((early, late, filters))
+    early = permuted(early, straight)
+    late = permuted(late, aside)
     earlier = permuted(cur, [(i, i + 1) for i in near])
     later = permuted(grad, [(i + 1, i) for i in near])
     matrices = circulants(filters)
-    earlier, late, matrices = lax.optimization_barrier((earlier, late, matrices))
-    late = permuted(late, onward)
+    late = permuted(jnp.where((x == 0) | last, jnp.zeros_like(late), late), onward)
     conv, back, lagged, diagonal = main_part(place, earlier, cur, grad, later, matrices, skip)
     early, lagged = lax.optimization_barrier((early, lagged))
-    lagged = far_lag(place, early, cur, grad, lagged)
-    conv, back = far_fix(0, place, early, cur, grad, matrices, skip, conv, back)
-    lagged, conv, back = lax.optimization_barrier((lagged, conv, back))
+    conv, back, lagged = far_fix(place, early, cur, grad, matrices, skip, conv, back, lagged)
     sent = in_order(over_plane, lagged, diagonal)
     late, sent = lax.optimization_barrier((late, sent))
     late = permuted(late, home)
     sums = in_order(over_column, sent)
-    conv, back = far_fix(1, place, late, cur, grad, matrices, skip, conv, back)
+    conv, back = far_fix(place, late, cur, grad, matrices, skip, conv, back)
     cut = sums.shape[0] - cur.shape[1] // (ctx * lax.axis_size("dp"))
     grad_filters = sums[:cut].reshape(-1, TAPS // lax.axis_size("dp")) / math.sqrt(token_total * CH)
     grad_skip = sums[cut:] / math.sqrt(token_total)

time: 136 us -> 132 us (0.971)
  the two profiles are of different devices: /device:TPU:2 before, /device:TPU:1 now
where the time goes in v2:
time: 132 us; the launch traced here: 131 us
  blocking collectives  75 us (57%)
  Pallas kernels  21.4 us (16%)
  starting transfers between devices  10.3 us (8%)
  local copies, waits for them, and re-layouts  9.82 us (7%)
  waiting for transfers between devices  9.55 us (7%)
  other arithmetic  4.46 us (3%)
    all_to_all x1, blocking collectives, over_plane(): lax.all_to_all(sent, 'ctx', 0, 0, axis_index_groups=pairs, tiled=True)  43.3 us
    all_to_all x1, blocking collectives, over_column(): lax.all_to_all(sent, ('dp', 'ctx'), 0, 0, axis_index_groups=columns, tile...  31.7 us
    ppermute x6, starting transfers between devices, permuted(): return lax.ppermute(array, 'ctx', pairs)  10.3 us
    pallas_call x2, Pallas kernels, far_fix(): pl.pallas_call(far_fix_kernel, grid_spec=pltpu.PrefetchScalarGridSpec(num...  9.68 us
    ppermute x6, waiting for transfers between devices, permuted(): return lax.ppermute(array, 'ctx', pairs)  9.55 us
    unnamed x14, local copies, waits for them, and re-layouts  8.27 us
    pallas_call x1, Pallas kernels, main_part(): pl.pallas_call(main_kernel, grid_spec=pltpu.PrefetchScalarGridSpec(num_sc...  7.74 us
    pallas_call x1, Pallas kernels, circulants(): pl.pallas_call(circulant_kernel, grid=(groups // step,), in_specs=[pl.Blo...  3.97 us
  transfers between devices with their start and end apart: 6, of which 2 were waited for; matrix products, arithmetic and copies ran while one was open for 2% of the time, Pallas kernels for 13%

profile of v2, /device:TPU:1, one launch (start us, length us, event | category | flops | bytes accessed | tf_op | source)
XLA Modules:
  0.0 131.4 jit_solution(3613921283006628805)
XLA Ops:
  0.7 2.7 %slice_select_fusion = (bf16[128,2048]{1,0:T(8,128)(2,1)}, bf16[128,2048]{1,0:T(8,128)(2,1)}) fusion(bf16[128,4096]{1,0:T(8,128)(2,1)} %bitcast.18, bf16[128,4096]{1,0:T(8,128)(2,1)} %bitcast.24, pred[]{:T(512)S(6)} %eq.9), kind=kLoop, calls=%fused_computation.2 | loop fusion | flops 524288 | bytes 3145729 | tf_op jit(solution)/shard_map/jit(_where)/select_n | solution.py:331
  3.4 1.4 %collective-permute-start = (bf16[128,2048]{1,0:T(8,128)(2,1)}, bf16[128,2048]{1,0:T(8,128)(2,1)}, u32[]{:S(2)}, u32[]{:S(2)}) collective-permute-start(bf16[128,2048]{1,0:T(8,128)(2,1)} %get-tuple-element.33), channel_id=1, source_target_pairs={{3,2},{7,6},{11,10},{15,14},{19,18},{23,22},{27,26},{4,5},{8,9},{1... | collective-permute-start | bytes 1572872 | tf_op jit(solution)/shard_map/ppermute | solution.py:311
  4.9 4.0 %collective-permute-start.3 = (bf16[128,4096]{1,0:T(8,128)(2,1)}, bf16[128,4096]{1,0:T(8,128)(2,1)S(1)}, u32[]{:S(2)}, u32[]{:S(2)}) collective-permute-start(bf16[128,4096]{1,0:T(8,128)(2,1)} %bitcast.25), channel_id=1, source_target_pairs={{0,1},{1,2},{2,3},{4,5},{5,6},{6,7},{8,9},{9,10},{10,11},{12,13},{... | collective-permute-start | bytes 3145736 | tf_op jit(solution)/shard_map/ppermute | solution.py:311
  8.9 1.3 collective-permute-start.4
  10.2 1.5 %collective-permute-start.2 = (bf16[128,2048]{1,0:T(8,128)(2,1)}, bf16[128,2048]{1,0:T(8,128)(2,1)}, u32[]{:S(2)}, u32[]{:S(2)}) collective-permute-start(bf16[128,2048]{1,0:T(8,128)(2,1)} %get-tuple-element.34), channel_id=1, source_target_pairs={{3,4},{7,8},{11,12},{15,16},{19,20},{23,24},{27,28},{4,3},{8,7},{1... | collective-permute-start | bytes 1572872 | tf_op jit(solution)/shard_map/ppermute | solution.py:311
  11.6 0.8 broadcast_select_fusion
  12.5 1.4 %collective-permute-start.1 = (bf16[128,2048]{1,0:T(8,128)(2,1)}, bf16[128,2048]{1,0:T(8,128)(2,1)}, u32[]{:S(2)}, u32[]{:S(2)}) collective-permute-start(bf16[128,2048]{1,0:T(8,128)(2,1)} %broadcast_select_fusion), channel_id=1, source_target_pairs={{2,5},{6,9},{10,13},{14,17},{18,21},{22,25},{26,29},{5,2},{9,6},{1... | collective-permute-start | bytes 1572872 | tf_op jit(solution)/shard_map/ppermute | solution.py:311
  13.9 0.8 copy-done.5
  14.8 4.0 %circulants.1 = bf16[2,256,64,128]{3,2,1,0:T(8,128)(2,1)S(1)} custom-call(bf16[256,128]{1,0:T(8,128)(2,1)S(1)} %copy-done.5), custom_call_target="tpu_custom_call" | custom-call | flops 1 | bytes 1 | tf_op jit(solution)/shard_map/circulants/pallas_call | solution.py:53
  18.8 3.2 %copy-done = bf16[2,256,64,128]{3,2,1,0:T(8,128)(2,1)} copy-done((bf16[2,256,64,128]{3,2,1,0:T(8,128)(2,1)}, bf16[2,256,64,128]{3,2,1,0:T(8,128)(2,1)S(1)}, u32[]{:S(2)}) %copy-start) | copy-done | bytes 8388632
  22.0 5.6 %collective-permute-done.3.earlier_ref = bf16[128,4096]{1,0:T(8,128)(2,1)S(1)} collective-permute-done((bf16[128,4096]{1,0:T(8,128)(2,1)}, bf16[128,4096]{1,0:T(8,128)(2,1)S(1)}, u32[]{:S(2)}, u32[]{:S(2)}) %collective-permute-start.3) | collective-permute-done | bytes 1048608 | tf_op jit(solution)/shard_map/ppermute | solution.py:311
  27.6 3.9 %collective-permute-done.4.later_ref = bf16[128,4096]{1,0:T(8,128)(2,1)} collective-permute-done((bf16[128,4096]{1,0:T(8,128)(2,1)}, bf16[128,4096]{1,0:T(8,128)(2,1)}, u32[]{:S(2)}, u32[]{:S(2)}) %collective-permute-start.4) | collective-permute-done | bytes 1048608 | tf_op jit(solution)/shard_map/ppermute | solution.py:311
  31.5 3.4 %copy-done.1 = bf16[2,256,64,128]{3,2,1,0:T(8,128)(2,1)S(1)} copy-done((bf16[2,256,64,128]{3,2,1,0:T(8,128)(2,1)S(1)}, bf16[2,256,64,128]{3,2,1,0:T(8,128)(2,1)}, u32[]{:S(2)}) %copy-start.1) | copy-done | bytes 8388632
  34.9 7.7 %main_part.1 = (bf16[128,4096]{1,0:T(8,128)(2,1)}, bf16[128,4096]{1,0:T(8,128)(2,1)}, f32[256,128]{1,0:T(8,128)S(1)}, f32[1,4096]{1,0:T(1,128)S(1)}) custom-call(s32[1]{0:T(128)} %bitcast.4.place_ref, bf16[128,4096]{1,0:T(8,128)(2,1)S(1)} %collective-permute-done.3.earlier_ref, bf16[128,4096]{1,0:T(8,128)(2,1)S(1)} %bitcast.27, ...), custom_call_target="tpu_custom_call" | custom-call | flops 1 | bytes 1 | tf_op jit(solution)/shard_map/main_part/pallas_call | solution.py:161
  42.7 5.6 %early_fix.1 = (bf16[128,4096]{1,0:T(8,128)(2,1)}, bf16[128,4096]{1,0:T(8,128)(2,1)}, f32[256,128]{1,0:T(8,128)S(1)}) custom-call(s32[1]{0:T(128)} %bitcast.4.place_ref, bf16[128,2048]{1,0:T(8,128)(2,1)} %collective-permute-done.2.halo_ref, bf16[128,4096]{1,0:T(8,128)(2,1)S(1)} %bitcast.28, ...), custom_call_target="tpu_custom_call", output_to_operand_aliasing={{0}: (7, {}), {1}: (8, {}), {2}: (11, {})} | custom-call | flops 1 | bytes 1 | tf_op jit(solution)/shard_map/early_fix/pallas_call | solution.py:269
  48.3 44.5 %conditional.2 = (f32[32,72]{1,0:T(8,128)S(1)}) conditional(s32[]{:T(128)} %convert_element_type.4, () %tuple.24, (f32[256,128]{1,0:T(8,128)S(1)}, f32[1,4096]{1,0:T(1,128)S(1)}) %tuple.26), branch_computations={%region_0.1_spmd, %region_1.3_spmd} | conditional | flops 73728 | bytes 1721356 | solution.py:307
  48.8 43.3 %all_to_all.15 = f32[16,1,2304]{2,1,0:T(1,128)S(1)} all-to-all(f32[16,1,2304]{2,1,0:T(1,128)S(1)} %all_to_all.12), channel_id=1, replica_groups={{0,1,2,3,8,9,10,11,16,17,18,19,24,25,26,27},{4,5,6,7,12,13,14,15,20,21,..., dimensions={0} | all-to-all | bytes 294912 | tf_op jit(solution)/shard_map/cond/branch_1_fun/all_to_all | solution.py:287
  92.8 0.7 collective-permute-start.5
  93.5 31.8 %conditional.3 = (f32[72]{0:T(128)S(1)}) conditional(s32[]{:T(128)} %convert_element_type.4, () %tuple.28, f32[32,72]{1,0:T(8,128)S(1)} %get-tuple-element.51), branch_computations={%region_3.4_spmd, %region_4.6_spmd} | conditional | flops 2232 | bytes 27948 | solution.py:307
  93.5 31.7 %all_to_all.16 = f32[32,1,72]{2,1,0:T(1,128)S(1)} all-to-all(f32[32,1,72]{2,1,0:T(1,128)S(1)} %bitcast.38), channel_id=1, replica_groups={{0,32,64,96,128,160,192,224,256,288,320,352,384,416,448,480,4,36,68,100..., dimensions={0} | all-to-all | bytes 18432 | tf_op jit(solution)/shard_map/cond/branch_1_fun/all_to_all | solution.py:300
  125.3 0.7 div.13
  125.9 0.6 slice_multiply_fusion
  126.5 0.8 copy-done.6
  127.3 4.1 %late_fix.1 = (bf16[128,4096]{1,0:T(8,128)(2,1)}, bf16[128,4096]{1,0:T(8,128)(2,1)}) custom-call(s32[1]{0:T(128)} %bitcast.4.place_ref, bf16[128,2048]{1,0:T(8,128)(2,1)} %copy-done.6, bf16[128,4096]{1,0:T(8,128)(2,1)} %bitcast.26, bf16[128,4096]{1,0:T(8,128)(2,1)} %bitcast.20, ...), custom_call_target="tpu_custom_call", output_to_operand_aliasing={{0}: (7, {}), {1}: (8, {})} | custom-call | flops 1 | bytes 1 | tf_op jit(solution)/shard_map/late_fix/pallas_call | solution.py:269
  (31 shorter events, 1.2 us)
Async XLA Ops:
  0.6 30.9 %copy-start.2 = (bf16[1,128,4096]{2,1,0:T(8,128)(2,1)S(1)}, bf16[1,128,4096]{2,1,0:T(8,128)(2,1)}, u32[]{:S(2)}) copy-start(bf16[1,128,4096]{2,1,0:T(8,128)(2,1)} %param.9) | copy-start | bytes 3145732
  0.6 30.9 %copy-start.3 = (bf16[1,128,4096]{2,1,0:T(8,128)(2,1)S(1)}, bf16[1,128,4096]{2,1,0:T(8,128)(2,1)}, u32[]{:S(2)}) copy-start(bf16[1,128,4096]{2,1,0:T(8,128)(2,1)} %param.8) | copy-start | bytes 3145732
  0.7 30.9 %copy-start.4 = (f32[4096]{0:T(1024)S(1)}, f32[4096]{0:T(1024)}, u32[]{:S(2)}) copy-start(f32[4096]{0:T(1024)} %param.11) | copy-start | bytes 49156
  3.4 8.2 %collective-permute-start = (bf16[128,2048]{1,0:T(8,128)(2,1)}, bf16[128,2048]{1,0:T(8,128)(2,1)}, u32[]{:S(2)}, u32[]{:S(2)}) collective-permute-start(bf16[128,2048]{1,0:T(8,128)(2,1)} %get-tuple-element.33), channel_id=1, source_target_pairs={{3,2},{7,6},{11,10},{15,14},{19,18},{23,22},{27,26},{4,5},{8,9},{1... | collective-permute-start | bytes 1572872 | tf_op jit(solution)/shard_map/ppermute | solution.py:311
  4.9 22.7 %collective-permute-start.3 = (bf16[128,4096]{1,0:T(8,128)(2,1)}, bf16[128,4096]{1,0:T(8,128)(2,1)S(1)}, u32[]{:S(2)}, u32[]{:S(2)}) collective-permute-start(bf16[128,4096]{1,0:T(8,128)(2,1)} %bitcast.25), channel_id=1, source_target_pairs={{0,1},{1,2},{2,3},{4,5},{5,6},{6,7},{8,9},{9,10},{10,11},{12,13},{... | collective-permute-start | bytes 3145736 | tf_op jit(solution)/shard_map/ppermute | solution.py:311
  8.9 22.6 %collective-permute-start.4 = (bf16[128,4096]{1,0:T(8,128)(2,1)}, bf16[128,4096]{1,0:T(8,128)(2,1)}, u32[]{:S(2)}, u32[]{:S(2)}) collective-permute-start(bf16[128,4096]{1,0:T(8,128)(2,1)} %bitcast.19), channel_id=1, source_target_pairs={{1,0},{2,1},{3,2},{5,4},{6,5},{7,6},{9,8},{10,9},{11,10},{13,12},{... | collective-permute-start | bytes 3145736 | tf_op jit(solution)/shard_map/ppermute | solution.py:311
  10.2 32.5 %collective-permute-start.2 = (bf16[128,2048]{1,0:T(8,128)(2,1)}, bf16[128,2048]{1,0:T(8,128)(2,1)}, u32[]{:S(2)}, u32[]{:S(2)}) collective-permute-start(bf16[128,2048]{1,0:T(8,128)(2,1)} %get-tuple-element.34), channel_id=1, source_target_pairs={{3,4},{7,8},{11,12},{15,16},{19,20},{23,24},{27,28},{4,3},{8,7},{1... | collective-permute-start | bytes 1572872 | tf_op jit(solution)/shard_map/ppermute | solution.py:311
  12.5 80.3 %collective-permute-start.1 = (bf16[128,2048]{1,0:T(8,128)(2,1)}, bf16[128,2048]{1,0:T(8,128)(2,1)}, u32[]{:S(2)}, u32[]{:S(2)}) collective-permute-start(bf16[128,2048]{1,0:T(8,128)(2,1)} %broadcast_select_fusion), channel_id=1, source_target_pairs={{2,5},{6,9},{10,13},{14,17},{18,21},{22,25},{26,29},{5,2},{9,6},{1... | collective-permute-start | bytes 1572872 | tf_op jit(solution)/shard_map/ppermute | solution.py:311
  13.9 0.8 copy-start.5
  18.8 3.2 %copy-start = (bf16[2,256,64,128]{3,2,1,0:T(8,128)(2,1)}, bf16[2,256,64,128]{3,2,1,0:T(8,128)(2,1)S(1)}, u32[]{:S(2)}) copy-start(bf16[2,256,64,128]{3,2,1,0:T(8,128)(2,1)S(1)} %circulants.1) | copy-start | bytes 25165828
  31.5 3.4 %copy-start.1 = (bf16[2,256,64,128]{3,2,1,0:T(8,128)(2,1)S(1)}, bf16[2,256,64,128]{3,2,1,0:T(8,128)(2,1)}, u32[]{:S(2)}) copy-start(bf16[2,256,64,128]{3,2,1,0:T(8,128)(2,1)} %copy-done) | copy-start | bytes 25165828
  92.8 33.7 %collective-permute-start.5 = (bf16[128,2048]{1,0:T(8,128)(2,1)}, bf16[128,2048]{1,0:T(8,128)(2,1)S(1)}, u32[]{:S(2)}, u32[]{:S(2)}) collective-permute-start(bf16[128,2048]{1,0:T(8,128)(2,1)} %collective-permute-done.1), channel_id=1, source_target_pairs={{5,4},{9,8},{13,12},{17,16},{21,20},{25,24},{29,28},{2,3},{6,7},{1... | collective-permute-start | bytes 1572872 | tf_op jit(solution)/shard_map/ppermute | solution.py:311
  126.5 0.8 copy-start.6

commit v3 on v2

--- a/solution.py
+++ b/solution.py
@@ -130,10 +130,12 @@
     return slice(index * LANES, (index + 1) * LANES), slice(index * PER * HALF, (index + 1) * PER * HALF)
 
 
-def main_kernel(place_ref, earlier_ref, cur_ref, grad_ref, later_ref, fwd_ref, bwd_ref, skip_ref, conv_ref, back_ref, lag_ref, diag_ref):
-    for at_end, forward, own_ref, halo_ref, matrix_ref, out_ref in (
-        (0, True, cur_ref, earlier_ref, fwd_ref, conv_ref),
-        (ROW - 1, False, grad_ref, later_ref, bwd_ref, back_ref),
+def main_kernel(place_ref, earlier_lo_ref, earlier_hi_ref, cur_ref, grad_ref, later_lo_ref, later_hi_ref, fwd_ref, bwd_ref, skip_ref, conv_ref, back_ref, lag_ref, diag_ref):
+    lower = pl.program_id(0) == 0
+
+    for at_end, forward, own_ref, halo_refs, matrix_ref, out_ref in (
+        (0, True, cur_ref, (earlier_lo_ref, earlier_hi_ref), fwd_ref, conv_ref),
+        (ROW - 1, False, grad_ref, (later_lo_ref, later_hi_ref), bwd_ref, back_ref),
     ):
 
         @pl.when(place_ref[0] != at_end)
@@ -141,13 +143,15 @@
             mask = inside_mask(forward)
             for index in range(MAIN_TILES):
                 lanes, rows = tile_of(index)
-                own, halo = own_ref[:, lanes], halo_ref[:, lanes]
+                own = own_ref[:, lanes]
+                halo = jnp.where(lower, halo_refs[0][:, lanes], halo_refs[1][:, lanes])
                 out_ref[:, lanes] = convolved(forward, matrix_ref[0, rows], mask, own, halo, skip_ref[:, lanes])
 
     sums = []
     for index in range(MAIN_TILES):
         lanes, _ = tile_of(index)
-        earlier, cur, grad = (ref[:, lanes] for ref in (earlier_ref, cur_ref, grad_ref))
+        cur, grad = cur_ref[:, lanes], grad_ref[:, lanes]
+        earlier = jnp.where(lower, earlier_lo_ref[:, lanes], earlier_hi_ref[:, lanes])
         diag_ref[:, lanes] = jnp.sum(cur.astype(jnp.float32) * grad.astype(jnp.float32), axis=0, keepdims=True)
         sums.append(cross_sums(earlier, cur, grad))
     lag_ref[...] = by_lag(jnp.concatenate(sums, axis=0))
@@ -156,6 +160,7 @@
 def main_part(place, earlier, cur, grad, later, matrices, skip):
     tokens, chans = cur.shape
     spec = pl.BlockSpec((tokens, MAIN_WIDE), lambda i, place: (0, i))
+    half = pl.BlockSpec((tokens, MAIN_WIDE), lambda i, place: (0, 0))
     row_spec = pl.BlockSpec((1, MAIN_WIDE), lambda i, place: (0, i))
     narrow = jax.ShapeDtypeStruct((tokens, chans), jnp.bfloat16)
     return pl.pallas_call(
@@ -163,7 +168,7 @@
         grid_spec=pltpu.PrefetchScalarGridSpec(
             num_scalar_prefetch=1,
             grid=(chans // MAIN_WIDE,),
-            in_specs=[spec] * 4
+            in_specs=[half, half, spec, spec, half, half]
             + [
                 pl.BlockSpec((1, MAIN_TILES * PER * HALF, TAPS), lambda i, place: (0, i, 0)),
                 pl.BlockSpec((1, MAIN_TILES * PER * HALF, TAPS), lambda i, place: (1, i, 0)),
@@ -180,7 +185,7 @@
         compiler_params=params(40 * 1024 * 1024),
         cost_estimate=SHORT,
         name="main_part",
-    )(place, earlier, cur, grad, later, matrices, matrices, skip)
+    )(place, *earlier, cur, grad, *later, matrices, matrices, skip)
 
 
 def far_fix_kernel(place_ref, halo_ref, cur_ref, grad_ref, matrix_ref, fwd_skip_ref, bwd_skip_ref, conv_ref, back_ref, *refs):
@@ -332,8 +337,9 @@
     early, late, filters = lax.optimization_barrier((early, late, filters))
     early = permuted(early, straight)
     late = permuted(late, aside)
-    earlier = permuted(cur, [(i, i + 1) for i in near])
-    later = permuted(grad, [(i + 1, i) for i in near])
+    halves = slice(0, half), slice(half, 2 * half)
+    earlier = [permuted(cur[:, lanes], [(i, i + 1) for i in near]) for lanes in halves]
+    later = [permuted(grad[:, lanes], [(i + 1, i) for i in near]) for lanes in halves]
     matrices = circulants(filters)
     late = permuted(jnp.where((x == 0) | last, jnp.zeros_like(late), late), onward)
     conv, back, lagged, diagonal = main_part(place, earlier, cur, grad, later, matrices, skip)

time: 132 us -> 127 us (0.962)
  blocking collectives: 75 us -> 56.2 us
  waiting for transfers between devices: 9.55 us -> 17.4 us
  starting transfers between devices: 10.3 us -> 15.6 us
    all_to_all x1, blocking collectives: 43.3 us -> 21.4 us  [over_plane(): lax.all_to_all(sent, 'ctx', 0, 0, axis_index_groups=pairs, tiled=True)]
    ppermute x6 -> x8, waiting for transfers between devices: 9.55 us -> 17.4 us  [permuted(): return lax.ppermute(array, 'ctx', pairs)]
    ppermute x6 -> x8, starting transfers between devices: 10.3 us -> 15.6 us  [permuted(): return lax.ppermute(array, 'ctx', pairs)]
    all_to_all x1, blocking collectives: 31.7 us -> 34.8 us  [over_column(): lax.all_to_all(sent, ('dp', 'ctx'), 0, 0, axis_index_groups=columns, tile...]
  transfers between devices with their start and end apart: 6 -> 8, of which waited for: 2 -> 2; matrix products, arithmetic and copies ran while one was open for 2% -> 2% of each run, Pallas kernels for 13% -> 14%
where the time goes in v3:
time: 127 us
  blocking collectives  56.2 us (44%)
  Pallas kernels  21.8 us (17%)
  waiting for transfers between devices  17.4 us (14%)
  starting transfers between devices  15.6 us (12%)
  local copies, waits for them, and re-layouts  9.84 us (8%)
  other arithmetic  5.14 us (4%)
    all_to_all x1, blocking collectives, over_column(): lax.all_to_all(sent, ('dp', 'ctx'), 0, 0, axis_index_groups=columns, tile...  34.8 us
    all_to_all x1, blocking collectives, over_plane(): lax.all_to_all(sent, 'ctx', 0, 0, axis_index_groups=pairs, tiled=True)  21.4 us
    ppermute x8, waiting for transfers between devices, permuted(): return lax.ppermute(array, 'ctx', pairs)  17.4 us
    ppermute x8, starting transfers between devices, permuted(): return lax.ppermute(array, 'ctx', pairs)  15.6 us
    pallas_call x2, Pallas kernels, far_fix(): pl.pallas_call(far_fix_kernel, grid_spec=pltpu.PrefetchScalarGridSpec(num...  9.66 us
    unnamed x14, local copies, waits for them, and re-layouts  8.29 us
    pallas_call x1, Pallas kernels, main_part(): pl.pallas_call(main_kernel, grid_spec=pltpu.PrefetchScalarGridSpec(num_sc...  8.14 us
    pallas_call x1, Pallas kernels, circulants(): pl.pallas_call(circulant_kernel, grid=(groups // step,), in_specs=[pl.Blo...  3.97 us
  transfers between devices with their start and end apart: 8, of which 2 were waited for; matrix products, arithmetic and copies ran while one was open for 2% of the time, Pallas kernels for 14%

profile of v3, /device:TPU:1, one launch (start us, length us, event | category | flops | bytes accessed | tf_op | source)
XLA Modules:
  0.0 126.7 jit_solution(14088164265781066293)
XLA Ops:
  0.7 3.4 %broadcast_select_fusion = (bf16[128,2048]{1,0:T(8,128)(2,1)}, bf16[128,2048]{1,0:T(8,128)(2,1)}, bf16[128,2048]{1,0:T(8,128)(2,1)}, bf16[128,2048]{1,0:T(8,128)...) fusion(pred[]{:T(512)S(6)} %eq.9, bf16[128,4096]{1,0:T(8,128)(2,1)} %bitcast.18, bf16[128,4096]{1,0:T(8,128)(2,1)} %bitcast.23), kind=kLoop, calls=%fused_computation.2 | loop fusion | flops 524288 | bytes 5242881 | tf_op jit(solution)/shard_map/jit(_where)/select_n | solution.py:336
  4.1 1.4 %collective-permute-start = (bf16[128,2048]{1,0:T(8,128)(2,1)}, bf16[128,2048]{1,0:T(8,128)(2,1)}, u32[]{:S(2)}, u32[]{:S(2)}) collective-permute-start(bf16[128,2048]{1,0:T(8,128)(2,1)} %get-tuple-element.33), channel_id=1, source_target_pairs={{3,2},{7,6},{11,10},{15,14},{19,18},{23,22},{27,26},{4,5},{8,9},{1... | collective-permute-start | bytes 1572872 | tf_op jit(solution)/shard_map/ppermute | solution.py:316
  5.5 1.3 %collective-permute-start.6 = (bf16[128,2048]{1,0:T(8,128)(2,1)}, bf16[128,2048]{1,0:T(8,128)(2,1)S(1)}, u32[]{:S(2)}, u32[]{:S(2)}) collective-permute-start(bf16[128,2048]{1,0:T(8,128)(2,1)} %get-tuple-element.51), channel_id=1, source_target_pairs={{1,0},{2,1},{3,2},{5,4},{6,5},{7,6},{9,8},{10,9},{11,10},{13,12},{... | collective-permute-start | bytes 1572872 | tf_op jit(solution)/shard_map/ppermute | solution.py:316
  6.8 0.7 collective-permute-start.2
  7.5 5.4 %collective-permute-start.4 = (bf16[128,2048]{1,0:T(8,128)(2,1)}, bf16[128,2048]{1,0:T(8,128)(2,1)}, u32[]{:S(2)}, u32[]{:S(2)}) collective-permute-start(bf16[128,2048]{1,0:T(8,128)(2,1)} %get-tuple-element.52), channel_id=1, source_target_pairs={{0,1},{1,2},{2,3},{4,5},{5,6},{6,7},{8,9},{9,10},{10,11},{12,13},{... | collective-permute-start | bytes 1572872 | tf_op jit(solution)/shard_map/ppermute | solution.py:316
  12.9 3.4 %collective-permute-start.3 = (bf16[128,2048]{1,0:T(8,128)(2,1)}, bf16[128,2048]{1,0:T(8,128)(2,1)}, u32[]{:S(2)}, u32[]{:S(2)}) collective-permute-start(bf16[128,2048]{1,0:T(8,128)(2,1)} %get-tuple-element.53), channel_id=1, source_target_pairs={{0,1},{1,2},{2,3},{4,5},{5,6},{6,7},{8,9},{9,10},{10,11},{12,13},{... | collective-permute-start | bytes 1572872 | tf_op jit(solution)/shard_map/ppermute | solution.py:316
  16.3 1.3 %collective-permute-start.5 = (bf16[128,2048]{1,0:T(8,128)(2,1)}, bf16[128,2048]{1,0:T(8,128)(2,1)}, u32[]{:S(2)}, u32[]{:S(2)}) collective-permute-start(bf16[128,2048]{1,0:T(8,128)(2,1)} %get-tuple-element.54), channel_id=1, source_target_pairs={{1,0},{2,1},{3,2},{5,4},{6,5},{7,6},{9,8},{10,9},{11,10},{13,12},{... | collective-permute-start | bytes 1572872 | tf_op jit(solution)/shard_map/ppermute | solution.py:316
  17.6 0.8 broadcast_select_fusion.2
  18.4 1.4 %collective-permute-start.1 = (bf16[128,2048]{1,0:T(8,128)(2,1)}, bf16[128,2048]{1,0:T(8,128)(2,1)}, u32[]{:S(2)}, u32[]{:S(2)}) collective-permute-start(bf16[128,2048]{1,0:T(8,128)(2,1)} %broadcast_select_fusion.2), channel_id=1, source_target_pairs={{2,5},{6,9},{10,13},{14,17},{18,21},{22,25},{26,29},{5,2},{9,6},{1... | collective-permute-start | bytes 1572872 | tf_op jit(solution)/shard_map/ppermute | solution.py:316
  19.9 0.8 copy-done.5
  20.7 4.0 %circulants.1 = bf16[2,256,64,128]{3,2,1,0:T(8,128)(2,1)S(1)} custom-call(bf16[256,128]{1,0:T(8,128)(2,1)S(1)} %copy-done.5), custom_call_target="tpu_custom_call" | custom-call | flops 1 | bytes 1 | tf_op jit(solution)/shard_map/circulants/pallas_call | solution.py:53
  24.7 3.2 %copy-done = bf16[2,256,64,128]{3,2,1,0:T(8,128)(2,1)} copy-done((bf16[2,256,64,128]{3,2,1,0:T(8,128)(2,1)}, bf16[2,256,64,128]{3,2,1,0:T(8,128)(2,1)S(1)}, u32[]{:S(2)}) %copy-start) | copy-done | bytes 8388632
  28.3 17.0 %collective-permute-done.5.later_lo_ref = bf16[128,2048]{1,0:T(8,128)(2,1)} collective-permute-done((bf16[128,2048]{1,0:T(8,128)(2,1)}, bf16[128,2048]{1,0:T(8,128)(2,1)}, u32[]{:S(2)}, u32[]{:S(2)}) %collective-permute-start.5) | collective-permute-done | bytes 524320 | tf_op jit(solution)/shard_map/ppermute | solution.py:316
  45.3 3.4 %copy-done.1 = bf16[2,256,64,128]{3,2,1,0:T(8,128)(2,1)S(1)} copy-done((bf16[2,256,64,128]{3,2,1,0:T(8,128)(2,1)S(1)}, bf16[2,256,64,128]{3,2,1,0:T(8,128)(2,1)}, u32[]{:S(2)}) %copy-start.1) | copy-done | bytes 8388632
  48.7 8.1 %main_part.1 = (bf16[128,4096]{1,0:T(8,128)(2,1)}, bf16[128,4096]{1,0:T(8,128)(2,1)}, f32[256,128]{1,0:T(8,128)S(1)}, f32[1,4096]{1,0:T(1,128)S(1)}) custom-call(s32[1]{0:T(128)} %bitcast.4.place_ref, bf16[128,2048]{1,0:T(8,128)(2,1)} %collective-permute-done.3.earlier_lo_ref, bf16[128,2048]{1,0:T(8,128)(2,1)} %collective-permute-done.4.earlier_hi_ref, ...), custom_call_target="tpu_custom_call" | custom-call | flops 1 | bytes 1 | tf_op jit(solution)/shard_map/main_part/pallas_call | solution.py:166
  56.9 5.6 %early_fix.1 = (bf16[128,4096]{1,0:T(8,128)(2,1)}, bf16[128,4096]{1,0:T(8,128)(2,1)}, f32[256,128]{1,0:T(8,128)S(1)}) custom-call(s32[1]{0:T(128)} %bitcast.4.place_ref, bf16[128,2048]{1,0:T(8,128)(2,1)S(1)} %collective-permute-done.2.halo_ref, bf16[128,4096]{1,0:T(8,128)(2,1)S(1)} %bitcast.26, ...), custom_call_target="tpu_custom_call", output_to_operand_aliasing={{0}: (7, {}), {1}: (8, {}), {2}: (11, {})} | custom-call | flops 1 | bytes 1 | tf_op jit(solution)/shard_map/early_fix/pallas_call | solution.py:274
  62.5 22.6 %conditional.2 = (f32[32,72]{1,0:T(8,128)S(1)}) conditional(s32[]{:T(128)} %convert_element_type.4, () %tuple.24, (f32[256,128]{1,0:T(8,128)S(1)}, f32[1,4096]{1,0:T(1,128)S(1)}) %tuple.26), branch_computations={%region_0.1_spmd, %region_1.3_spmd} | conditional | flops 73728 | bytes 1721356 | solution.py:312
  63.0 21.4 %all_to_all.15 = f32[16,1,2304]{2,1,0:T(1,128)S(1)} all-to-all(f32[16,1,2304]{2,1,0:T(1,128)S(1)} %all_to_all.12), channel_id=1, replica_groups={{0,1,2,3,8,9,10,11,16,17,18,19,24,25,26,27},{4,5,6,7,12,13,14,15,20,21,..., dimensions={0} | all-to-all | bytes 294912 | tf_op jit(solution)/shard_map/cond/branch_1_fun/all_to_all | solution.py:292
  85.1 0.7 collective-permute-start.7
  85.8 34.8 %conditional.3 = (f32[72]{0:T(128)S(1)}) conditional(s32[]{:T(128)} %convert_element_type.4, () %tuple.28, f32[32,72]{1,0:T(8,128)S(1)} %get-tuple-element.55), branch_computations={%region_3.4_spmd, %region_4.6_spmd} | conditional | flops 2232 | bytes 27948 | solution.py:312
  85.8 34.8 %all_to_all.16 = f32[32,1,72]{2,1,0:T(1,128)S(1)} all-to-all(f32[32,1,72]{2,1,0:T(1,128)S(1)} %bitcast.36), channel_id=1, replica_groups={{0,32,64,96,128,160,192,224,256,288,320,352,384,416,448,480,4,36,68,100..., dimensions={0} | all-to-all | bytes 18432 | tf_op jit(solution)/shard_map/cond/branch_1_fun/all_to_all | solution.py:305
  120.6 0.7 div.13
  121.9 0.8 copy-done.6
  122.7 4.1 %late_fix.1 = (bf16[128,4096]{1,0:T(8,128)(2,1)}, bf16[128,4096]{1,0:T(8,128)(2,1)}) custom-call(s32[1]{0:T(128)} %bitcast.4.place_ref, bf16[128,2048]{1,0:T(8,128)(2,1)} %copy-done.6, bf16[128,4096]{1,0:T(8,128)(2,1)} %bitcast.24, bf16[128,4096]{1,0:T(8,128)(2,1)} %bitcast.19, ...), custom_call_target="tpu_custom_call", output_to_operand_aliasing={{0}: (7, {}), {1}: (8, {})} | custom-call | flops 1 | bytes 1 | tf_op jit(solution)/shard_map/late_fix/pallas_call | solution.py:274
  (35 shorter events, 2.2 us)
Async XLA Ops:
  0.6 44.7 %copy-start.2 = (bf16[1,128,4096]{2,1,0:T(8,128)(2,1)S(1)}, bf16[1,128,4096]{2,1,0:T(8,128)(2,1)}, u32[]{:S(2)}) copy-start(bf16[1,128,4096]{2,1,0:T(8,128)(2,1)} %param.9) | copy-start | bytes 3145732
  0.6 44.7 %copy-start.3 = (bf16[1,128,4096]{2,1,0:T(8,128)(2,1)S(1)}, bf16[1,128,4096]{2,1,0:T(8,128)(2,1)}, u32[]{:S(2)}) copy-start(bf16[1,128,4096]{2,1,0:T(8,128)(2,1)} %param.8) | copy-start | bytes 3145732
  0.7 44.7 %copy-start.4 = (f32[4096]{0:T(1024)S(1)}, f32[4096]{0:T(1024)}, u32[]{:S(2)}) copy-start(f32[4096]{0:T(1024)} %param.11) | copy-start | bytes 49156
  4.1 12.2 %collective-permute-start = (bf16[128,2048]{1,0:T(8,128)(2,1)}, bf16[128,2048]{1,0:T(8,128)(2,1)}, u32[]{:S(2)}, u32[]{:S(2)}) collective-permute-start(bf16[128,2048]{1,0:T(8,128)(2,1)} %get-tuple-element.33), channel_id=1, source_target_pairs={{3,2},{7,6},{11,10},{15,14},{19,18},{23,22},{27,26},{4,5},{8,9},{1... | collective-permute-start | bytes 1572872 | tf_op jit(solution)/shard_map/ppermute | solution.py:316
  5.5 12.9 %collective-permute-start.6 = (bf16[128,2048]{1,0:T(8,128)(2,1)}, bf16[128,2048]{1,0:T(8,128)(2,1)S(1)}, u32[]{:S(2)}, u32[]{:S(2)}) collective-permute-start(bf16[128,2048]{1,0:T(8,128)(2,1)} %get-tuple-element.51), channel_id=1, source_target_pairs={{1,0},{2,1},{3,2},{5,4},{6,5},{7,6},{9,8},{10,9},{11,10},{13,12},{... | collective-permute-start | bytes 1572872 | tf_op jit(solution)/shard_map/ppermute | solution.py:316
  6.8 50.0 %collective-permute-start.2 = (bf16[128,2048]{1,0:T(8,128)(2,1)}, bf16[128,2048]{1,0:T(8,128)(2,1)S(1)}, u32[]{:S(2)}, u32[]{:S(2)}) collective-permute-start(bf16[128,2048]{1,0:T(8,128)(2,1)} %get-tuple-element.34), channel_id=1, source_target_pairs={{3,4},{7,8},{11,12},{15,16},{19,20},{23,24},{27,28},{4,3},{8,7},{1... | collective-permute-start | bytes 1572872 | tf_op jit(solution)/shard_map/ppermute | solution.py:316
  7.5 20.4 %collective-permute-start.4 = (bf16[128,2048]{1,0:T(8,128)(2,1)}, bf16[128,2048]{1,0:T(8,128)(2,1)}, u32[]{:S(2)}, u32[]{:S(2)}) collective-permute-start(bf16[128,2048]{1,0:T(8,128)(2,1)} %get-tuple-element.52), channel_id=1, source_target_pairs={{0,1},{1,2},{2,3},{4,5},{5,6},{6,7},{8,9},{9,10},{10,11},{12,13},{... | collective-permute-start | bytes 1572872 | tf_op jit(solution)/shard_map/ppermute | solution.py:316
  12.9 15.4 %collective-permute-start.3 = (bf16[128,2048]{1,0:T(8,128)(2,1)}, bf16[128,2048]{1,0:T(8,128)(2,1)}, u32[]{:S(2)}, u32[]{:S(2)}) collective-permute-start(bf16[128,2048]{1,0:T(8,128)(2,1)} %get-tuple-element.53), channel_id=1, source_target_pairs={{0,1},{1,2},{2,3},{4,5},{5,6},{6,7},{8,9},{9,10},{10,11},{12,13},{... | collective-permute-start | bytes 1572872 | tf_op jit(solution)/shard_map/ppermute | solution.py:316
  16.3 29.0 %collective-permute-start.5 = (bf16[128,2048]{1,0:T(8,128)(2,1)}, bf16[128,2048]{1,0:T(8,128)(2,1)}, u32[]{:S(2)}, u32[]{:S(2)}) collective-permute-start(bf16[128,2048]{1,0:T(8,128)(2,1)} %get-tuple-element.54), channel_id=1, source_target_pairs={{1,0},{2,1},{3,2},{5,4},{6,5},{7,6},{9,8},{10,9},{11,10},{13,12},{... | collective-permute-start | bytes 1572872 | tf_op jit(solution)/shard_map/ppermute | solution.py:316
  18.4 66.6 %collective-permute-start.1 = (bf16[128,2048]{1,0:T(8,128)(2,1)}, bf16[128,2048]{1,0:T(8,128)(2,1)}, u32[]{:S(2)}, u32[]{:S(2)}) collective-permute-start(bf16[128,2048]{1,0:T(8,128)(2,1)} %broadcast_select_fusion.2), channel_id=1, source_target_pairs={{2,5},{6,9},{10,13},{14,17},{18,21},{22,25},{26,29},{5,2},{9,6},{1... | collective-permute-start | bytes 1572872 | tf_op jit(solution)/shard_map/ppermute | solution.py:316
  19.9 0.8 copy-start.5
  24.7 3.2 %copy-start = (bf16[2,256,64,128]{3,2,1,0:T(8,128)(2,1)}, bf16[2,256,64,128]{3,2,1,0:T(8,128)(2,1)S(1)}, u32[]{:S(2)}) copy-start(bf16[2,256,64,128]{3,2,1,0:T(8,128)(2,1)S(1)} %circulants.1) | copy-start | bytes 25165828
  45.3 3.4 %copy-start.1 = (bf16[2,256,64,128]{3,2,1,0:T(8,128)(2,1)S(1)}, bf16[2,256,64,128]{3,2,1,0:T(8,128)(2,1)}, u32[]{:S(2)}) copy-start(bf16[2,256,64,128]{3,2,1,0:T(8,128)(2,1)} %copy-done) | copy-start | bytes 25165828
  85.1 36.8 %collective-permute-start.7 = (bf16[128,2048]{1,0:T(8,128)(2,1)}, bf16[128,2048]{1,0:T(8,128)(2,1)S(1)}, u32[]{:S(2)}, u32[]{:S(2)}) collective-permute-start(bf16[128,2048]{1,0:T(8,128)(2,1)} %collective-permute-done.1), channel_id=1, source_target_pairs={{5,4},{9,8},{13,12},{17,16},{21,20},{25,24},{29,28},{2,3},{6,7},{1... | collective-permute-start | bytes 1572872 | tf_op jit(solution)/shard_map/ppermute | solution.py:316
  121.9 0.8 copy-start.6

commit v4 on v3

--- a/solution.py
+++ b/solution.py
@@ -19,7 +19,7 @@
 MAIN_TILES = 16
 MAIN_WIDE = MAIN_TILES * LANES
 ROW = 4
-LARGE, SMALL = 56 * 1024 * 1024, 24 * 1024 * 1024
+LARGE, SMALL = 51 * 1024 * 1024, 24 * 1024 * 1024
 SHORT = pl.CostEstimate(flops=1, bytes_accessed=1, transcendentals=0)
 
 
@@ -341,6 +341,7 @@
     earlier = [permuted(cur[:, lanes], [(i, i + 1) for i in near]) for lanes in halves]
     later = [permuted(grad[:, lanes], [(i + 1, i) for i in near]) for lanes in halves]
     matrices = circulants(filters)
+    late = lax.optimization_barrier(jnp.where((x == 0) | last, jnp.zeros_like(late), late))
     late = permuted(jnp.where((x == 0) | last, jnp.zeros_like(late), late), onward)
     conv, back, lagged, diagonal = main_part(place, earlier, cur, grad, later, matrices, skip)
     early, lagged = lax.optimization_barrier((early, lagged))

time: 127 us -> 125 us (0.984)
  blocking collectives: 56.2 us -> 54.8 us
    all_to_all x1, blocking collectives: 34.8 us -> 33.5 us  [over_column(): lax.all_to_all(sent, ('dp', 'ctx'), 0, 0, axis_index_groups=columns, tile...]
    unnamed x14 -> x12, local copies, waits for them, and re-layouts: 8.29 us -> 7.44 us
where the time goes in v4:
time: 125 us; the launch traced here: 124 us
  blocking collectives  54.8 us (44%)
  Pallas kernels  21.5 us (17%)
  waiting for transfers between devices  17.4 us (14%)
  starting transfers between devices  15.6 us (12%)
  local copies, waits for them, and re-layouts  8.98 us (7%)
  other arithmetic  5.19 us (4%)
    all_to_all x1, blocking collectives, over_column(): lax.all_to_all(sent, ('dp', 'ctx'), 0, 0, axis_index_groups=columns, tile...  33.5 us
    all_to_all x1, blocking collectives, over_plane(): lax.all_to_all(sent, 'ctx', 0, 0, axis_index_groups=pairs, tiled=True)  21.3 us
    ppermute x8, waiting for transfers between devices, permuted(): return lax.ppermute(array, 'ctx', pairs)  17.4 us
    ppermute x8, starting transfers between devices, permuted(): return lax.ppermute(array, 'ctx', pairs)  15.6 us
    pallas_call x2, Pallas kernels, far_fix(): pl.pallas_call(far_fix_kernel, grid_spec=pltpu.PrefetchScalarGridSpec(num...  9.42 us
    pallas_call x1, Pallas kernels, main_part(): pl.pallas_call(main_kernel, grid_spec=pltpu.PrefetchScalarGridSpec(num_sc...  8.15 us
    unnamed x12, local copies, waits for them, and re-layouts  7.44 us
    pallas_call x1, Pallas kernels, circulants(): pl.pallas_call(circulant_kernel, grid=(groups // step,), in_specs=[pl.Blo...  3.97 us
  transfers between devices with their start and end apart: 8, of which 2 were waited for; matrix products, arithmetic and copies ran while one was open for 2% of the time, Pallas kernels for 14%

profile of v4, /device:TPU:1, one launch (start us, length us, event | category | flops | bytes accessed | tf_op | source)
XLA Modules:
  0.0 124.4 jit_solution(9016157201923891622)
XLA Ops:
  0.7 3.4 %broadcast_select_fusion = (bf16[128,2048]{1,0:T(8,128)(2,1)}, bf16[128,2048]{1,0:T(8,128)(2,1)}, bf16[128,2048]{1,0:T(8,128)(2,1)}, bf16[128,2048]{1,0:T(8,128)...) fusion(pred[]{:T(512)S(6)} %eq.10, bf16[128,4096]{1,0:T(8,128)(2,1)} %bitcast.18, bf16[128,4096]{1,0:T(8,128)(2,1)} %bitcast.23), kind=kLoop, calls=%fused_computation.2 | loop fusion | flops 524288 | bytes 5242881 | tf_op jit(solution)/shard_map/jit(_where)/select_n | solution.py:336
  4.1 1.5 %collective-permute-start = (bf16[128,2048]{1,0:T(8,128)(2,1)}, bf16[128,2048]{1,0:T(8,128)(2,1)}, u32[]{:S(2)}, u32[]{:S(2)}) collective-permute-start(bf16[128,2048]{1,0:T(8,128)(2,1)} %get-tuple-element.33), channel_id=1, source_target_pairs={{3,2},{7,6},{11,10},{15,14},{19,18},{23,22},{27,26},{4,5},{8,9},{1... | collective-permute-start | bytes 1572872 | tf_op jit(solution)/shard_map/ppermute | solution.py:316
  5.5 0.7 collective-permute-start.2
  6.2 1.3 %collective-permute-start.6 = (bf16[128,2048]{1,0:T(8,128)(2,1)}, bf16[128,2048]{1,0:T(8,128)(2,1)S(1)}, u32[]{:S(2)}, u32[]{:S(2)}) collective-permute-start(bf16[128,2048]{1,0:T(8,128)(2,1)} %get-tuple-element.51), channel_id=1, source_target_pairs={{1,0},{2,1},{3,2},{5,4},{6,5},{7,6},{9,8},{10,9},{11,10},{13,12},{... | collective-permute-start | bytes 1572872 | tf_op jit(solution)/shard_map/ppermute | solution.py:316
  7.5 5.4 %collective-permute-start.4 = (bf16[128,2048]{1,0:T(8,128)(2,1)}, bf16[128,2048]{1,0:T(8,128)(2,1)}, u32[]{:S(2)}, u32[]{:S(2)}) collective-permute-start(bf16[128,2048]{1,0:T(8,128)(2,1)} %get-tuple-element.52), channel_id=1, source_target_pairs={{0,1},{1,2},{2,3},{4,5},{5,6},{6,7},{8,9},{9,10},{10,11},{12,13},{... | collective-permute-start | bytes 1572872 | tf_op jit(solution)/shard_map/ppermute | solution.py:316
  12.9 3.4 %collective-permute-start.3 = (bf16[128,2048]{1,0:T(8,128)(2,1)}, bf16[128,2048]{1,0:T(8,128)(2,1)}, u32[]{:S(2)}, u32[]{:S(2)}) collective-permute-start(bf16[128,2048]{1,0:T(8,128)(2,1)} %get-tuple-element.53), channel_id=1, source_target_pairs={{0,1},{1,2},{2,3},{4,5},{5,6},{6,7},{8,9},{9,10},{10,11},{12,13},{... | collective-permute-start | bytes 1572872 | tf_op jit(solution)/shard_map/ppermute | solution.py:316
  16.3 1.3 %collective-permute-start.5 = (bf16[128,2048]{1,0:T(8,128)(2,1)}, bf16[128,2048]{1,0:T(8,128)(2,1)}, u32[]{:S(2)}, u32[]{:S(2)}) collective-permute-start(bf16[128,2048]{1,0:T(8,128)(2,1)} %get-tuple-element.54), channel_id=1, source_target_pairs={{1,0},{2,1},{3,2},{5,4},{6,5},{7,6},{9,8},{10,9},{11,10},{13,12},{... | collective-permute-start | bytes 1572872 | tf_op jit(solution)/shard_map/ppermute | solution.py:316
  17.6 0.8 broadcast_select_fusion.2
  18.5 1.5 %collective-permute-start.1 = (bf16[128,2048]{1,0:T(8,128)(2,1)}, bf16[128,2048]{1,0:T(8,128)(2,1)}, u32[]{:S(2)}, u32[]{:S(2)}) collective-permute-start(bf16[128,2048]{1,0:T(8,128)(2,1)} %broadcast_select_fusion.2), channel_id=1, source_target_pairs={{2,5},{6,9},{10,13},{14,17},{18,21},{22,25},{26,29},{5,2},{9,6},{1... | collective-permute-start | bytes 1572872 | tf_op jit(solution)/shard_map/ppermute | solution.py:316
  19.9 0.8 copy-done.5
  20.8 4.0 %circulants.1 = bf16[2,256,64,128]{3,2,1,0:T(8,128)(2,1)S(1)} custom-call(bf16[256,128]{1,0:T(8,128)(2,1)S(1)} %copy-done.5), custom_call_target="tpu_custom_call" | custom-call | flops 1 | bytes 1 | tf_op jit(solution)/shard_map/circulants/pallas_call | solution.py:53
  24.8 3.2 %copy-done = bf16[2,256,64,128]{3,2,1,0:T(8,128)(2,1)} copy-done((bf16[2,256,64,128]{3,2,1,0:T(8,128)(2,1)}, bf16[2,256,64,128]{3,2,1,0:T(8,128)(2,1)S(1)}, u32[]{:S(2)}) %copy-start) | copy-done | bytes 8388632
  28.3 17.1 %collective-permute-done.5.later_lo_ref = bf16[128,2048]{1,0:T(8,128)(2,1)} collective-permute-done((bf16[128,2048]{1,0:T(8,128)(2,1)}, bf16[128,2048]{1,0:T(8,128)(2,1)}, u32[]{:S(2)}, u32[]{:S(2)}) %collective-permute-start.5) | collective-permute-done | bytes 524320 | tf_op jit(solution)/shard_map/ppermute | solution.py:316
  45.4 3.4 %copy-done.1 = bf16[2,256,64,128]{3,2,1,0:T(8,128)(2,1)S(1)} copy-done((bf16[2,256,64,128]{3,2,1,0:T(8,128)(2,1)S(1)}, bf16[2,256,64,128]{3,2,1,0:T(8,128)(2,1)}, u32[]{:S(2)}) %copy-start.1) | copy-done | bytes 8388632
  48.8 8.1 %main_part.1 = (bf16[128,4096]{1,0:T(8,128)(2,1)}, bf16[128,4096]{1,0:T(8,128)(2,1)}, f32[256,128]{1,0:T(8,128)S(1)}, f32[1,4096]{1,0:T(1,128)S(1)}) custom-call(s32[1]{0:T(128)} %bitcast.4.place_ref, bf16[128,2048]{1,0:T(8,128)(2,1)} %collective-permute-done.3.earlier_lo_ref, bf16[128,2048]{1,0:T(8,128)(2,1)} %collective-permute-done.4.earlier_hi_ref, ...), custom_call_target="tpu_custom_call" | custom-call | flops 1 | bytes 1 | tf_op jit(solution)/shard_map/main_part/pallas_call | solution.py:166
  56.9 5.6 %early_fix.1 = (bf16[128,4096]{1,0:T(8,128)(2,1)}, bf16[128,4096]{1,0:T(8,128)(2,1)}, f32[256,128]{1,0:T(8,128)S(1)}) custom-call(s32[1]{0:T(128)} %bitcast.4.place_ref, bf16[128,2048]{1,0:T(8,128)(2,1)S(1)} %collective-permute-done.2.halo_ref, bf16[128,4096]{1,0:T(8,128)(2,1)S(1)} %bitcast.25, ...), custom_call_target="tpu_custom_call", output_to_operand_aliasing={{0}: (7, {}), {1}: (8, {}), {2}: (11, {})} | custom-call | flops 1 | bytes 1 | tf_op jit(solution)/shard_map/early_fix/pallas_call | solution.py:274
  62.5 22.5 %conditional.2 = (f32[32,72]{1,0:T(8,128)S(1)}) conditional(s32[]{:T(128)} %convert_element_type.4, () %tuple.24, (f32[256,128]{1,0:T(8,128)S(1)}, f32[1,4096]{1,0:T(1,128)S(1)}) %tuple.26), branch_computations={%region_0.1_spmd, %region_1.3_spmd} | conditional | flops 73728 | bytes 1721356 | solution.py:312
  63.0 21.3 %all_to_all.15 = f32[16,1,2304]{2,1,0:T(1,128)S(1)} all-to-all(f32[16,1,2304]{2,1,0:T(1,128)S(1)} %all_to_all.12), channel_id=1, replica_groups={{0,1,2,3,8,9,10,11,16,17,18,19,24,25,26,27},{4,5,6,7,12,13,14,15,20,21,..., dimensions={0} | all-to-all | bytes 294912 | tf_op jit(solution)/shard_map/cond/branch_1_fun/all_to_all | solution.py:292
  85.0 0.7 collective-permute-start.7
  85.7 33.5 %conditional.3 = (f32[72]{0:T(128)S(1)}) conditional(s32[]{:T(128)} %convert_element_type.4, () %tuple.28, f32[32,72]{1,0:T(8,128)S(1)} %get-tuple-element.55), branch_computations={%region_3.4_spmd, %region_4.6_spmd} | conditional | flops 2232 | bytes 27948 | solution.py:312
  85.8 33.5 %all_to_all.16 = f32[32,1,72]{2,1,0:T(1,128)S(1)} all-to-all(f32[32,1,72]{2,1,0:T(1,128)S(1)} %bitcast.36), channel_id=1, replica_groups={{0,32,64,96,128,160,192,224,256,288,320,352,384,416,448,480,4,36,68,100..., dimensions={0} | all-to-all | bytes 18432 | tf_op jit(solution)/shard_map/cond/branch_1_fun/all_to_all | solution.py:305
  119.3 0.7 div.13
  120.0 0.6 slice_multiply_fusion
  120.5 3.8 %late_fix.1 = (bf16[128,4096]{1,0:T(8,128)(2,1)}, bf16[128,4096]{1,0:T(8,128)(2,1)}) custom-call(s32[1]{0:T(128)} %bitcast.4.place_ref, bf16[128,2048]{1,0:T(8,128)(2,1)S(1)} %collective-permute-done.7.halo_ref, bf16[128,4096]{1,0:T(8,128)(2,1)S(1)} %bitcast.27, bf16[128,4096]{1,0:T(8,128)(2,1)S(1)} %bitcast.22, ...), custom_call_target="tpu_custom_call", output_to_operand_aliasing={{0}: (7, {}), {1}: (8, {})} | custom-call | flops 1 | bytes 1 | tf_op jit(solution)/shard_map/late_fix/pallas_call | solution.py:274
  (34 shorter events, 1.6 us)
Async XLA Ops:
  0.6 44.7 %copy-start.2 = (bf16[1,128,4096]{2,1,0:T(8,128)(2,1)S(1)}, bf16[1,128,4096]{2,1,0:T(8,128)(2,1)}, u32[]{:S(2)}) copy-start(bf16[1,128,4096]{2,1,0:T(8,128)(2,1)} %param.9) | copy-start | bytes 3145732
  0.6 44.7 %copy-start.3 = (bf16[1,128,4096]{2,1,0:T(8,128)(2,1)S(1)}, bf16[1,128,4096]{2,1,0:T(8,128)(2,1)}, u32[]{:S(2)}) copy-start(bf16[1,128,4096]{2,1,0:T(8,128)(2,1)} %param.8) | copy-start | bytes 3145732
  0.7 44.7 %copy-start.4 = (f32[4096]{0:T(1024)S(1)}, f32[4096]{0:T(1024)}, u32[]{:S(2)}) copy-start(f32[4096]{0:T(1024)} %param.11) | copy-start | bytes 49156
  4.1 12.2 %collective-permute-start = (bf16[128,2048]{1,0:T(8,128)(2,1)}, bf16[128,2048]{1,0:T(8,128)(2,1)}, u32[]{:S(2)}, u32[]{:S(2)}) collective-permute-start(bf16[128,2048]{1,0:T(8,128)(2,1)} %get-tuple-element.33), channel_id=1, source_target_pairs={{3,2},{7,6},{11,10},{15,14},{19,18},{23,22},{27,26},{4,5},{8,9},{1... | collective-permute-start | bytes 1572872 | tf_op jit(solution)/shard_map/ppermute | solution.py:316
  5.5 51.4 %collective-permute-start.2 = (bf16[128,2048]{1,0:T(8,128)(2,1)}, bf16[128,2048]{1,0:T(8,128)(2,1)S(1)}, u32[]{:S(2)}, u32[]{:S(2)}) collective-permute-start(bf16[128,2048]{1,0:T(8,128)(2,1)} %get-tuple-element.34), channel_id=1, source_target_pairs={{3,4},{7,8},{11,12},{15,16},{19,20},{23,24},{27,28},{4,3},{8,7},{1... | collective-permute-start | bytes 1572872 | tf_op jit(solution)/shard_map/ppermute | solution.py:316
  6.2 12.2 %collective-permute-start.6 = (bf16[128,2048]{1,0:T(8,128)(2,1)}, bf16[128,2048]{1,0:T(8,128)(2,1)S(1)}, u32[]{:S(2)}, u32[]{:S(2)}) collective-permute-start(bf16[128,2048]{1,0:T(8,128)(2,1)} %get-tuple-element.51), channel_id=1, source_target_pairs={{1,0},{2,1},{3,2},{5,4},{6,5},{7,6},{9,8},{10,9},{11,10},{13,12},{... | collective-permute-start | bytes 1572872 | tf_op jit(solution)/shard_map/ppermute | solution.py:316
  7.5 20.4 %collective-permute-start.4 = (bf16[128,2048]{1,0:T(8,128)(2,1)}, bf16[128,2048]{1,0:T(8,128)(2,1)}, u32[]{:S(2)}, u32[]{:S(2)}) collective-permute-start(bf16[128,2048]{1,0:T(8,128)(2,1)} %get-tuple-element.52), channel_id=1, source_target_pairs={{0,1},{1,2},{2,3},{4,5},{5,6},{6,7},{8,9},{9,10},{10,11},{12,13},{... | collective-permute-start | bytes 1572872 | tf_op jit(solution)/shard_map/ppermute | solution.py:316
  12.9 15.4 %collective-permute-start.3 = (bf16[128,2048]{1,0:T(8,128)(2,1)}, bf16[128,2048]{1,0:T(8,128)(2,1)}, u32[]{:S(2)}, u32[]{:S(2)}) collective-permute-start(bf16[128,2048]{1,0:T(8,128)(2,1)} %get-tuple-element.53), channel_id=1, source_target_pairs={{0,1},{1,2},{2,3},{4,5},{5,6},{6,7},{8,9},{9,10},{10,11},{12,13},{... | collective-permute-start | bytes 1572872 | tf_op jit(solution)/shard_map/ppermute | solution.py:316
  16.3 29.1 %collective-permute-start.5 = (bf16[128,2048]{1,0:T(8,128)(2,1)}, bf16[128,2048]{1,0:T(8,128)(2,1)}, u32[]{:S(2)}, u32[]{:S(2)}) collective-permute-start(bf16[128,2048]{1,0:T(8,128)(2,1)} %get-tuple-element.54), channel_id=1, source_target_pairs={{1,0},{2,1},{3,2},{5,4},{6,5},{7,6},{9,8},{10,9},{11,10},{13,12},{... | collective-permute-start | bytes 1572872 | tf_op jit(solution)/shard_map/ppermute | solution.py:316
  18.5 66.6 %collective-permute-start.1 = (bf16[128,2048]{1,0:T(8,128)(2,1)}, bf16[128,2048]{1,0:T(8,128)(2,1)}, u32[]{:S(2)}, u32[]{:S(2)}) collective-permute-start(bf16[128,2048]{1,0:T(8,128)(2,1)} %broadcast_select_fusion.2), channel_id=1, source_target_pairs={{2,5},{6,9},{10,13},{14,17},{18,21},{22,25},{26,29},{5,2},{9,6},{1... | collective-permute-start | bytes 1572872 | tf_op jit(solution)/shard_map/ppermute | solution.py:316
  19.9 0.8 copy-start.5
  24.8 3.2 %copy-start = (bf16[2,256,64,128]{3,2,1,0:T(8,128)(2,1)}, bf16[2,256,64,128]{3,2,1,0:T(8,128)(2,1)S(1)}, u32[]{:S(2)}) copy-start(bf16[2,256,64,128]{3,2,1,0:T(8,128)(2,1)S(1)} %circulants.1) | copy-start | bytes 25165828
  45.4 3.4 %copy-start.1 = (bf16[2,256,64,128]{3,2,1,0:T(8,128)(2,1)S(1)}, bf16[2,256,64,128]{3,2,1,0:T(8,128)(2,1)}, u32[]{:S(2)}) copy-start(bf16[2,256,64,128]{3,2,1,0:T(8,128)(2,1)} %copy-done) | copy-start | bytes 25165828
  85.0 35.5 %collective-permute-start.7 = (bf16[128,2048]{1,0:T(8,128)(2,1)}, bf16[128,2048]{1,0:T(8,128)(2,1)S(1)}, u32[]{:S(2)}, u32[]{:S(2)}) collective-permute-start(bf16[128,2048]{1,0:T(8,128)(2,1)} %collective-permute-done.1), channel_id=1, source_target_pairs={{5,4},{9,8},{13,12},{17,16},{21,20},{25,24},{29,28},{2,3},{6,7},{1... | collective-permute-start | bytes 1572872 | tf_op jit(solution)/shard_map/ppermute | solution.py:316

commit v5 on v4

--- a/solution.py
+++ b/solution.py
@@ -332,14 +332,15 @@
     home = [(i + 2, i + 1) for i in far] + [(i - 1, i) for i in far]
 
     last = x == ROW - 1
-    early = jnp.where(last, cur[:, :half], grad[:, half:])
     late = jnp.where(last, cur[:, half:], grad[:, :half])
-    early, late, filters = lax.optimization_barrier((early, late, filters))
+    cur_next, grad_next, late = lax.optimization_barrier((cur, grad, late))
+    early = jnp.where(last, cur_next[:, :half], grad_next[:, half:])
+    cur_next, grad_next, early, filters = lax.optimization_barrier((cur_next, grad_next, early, filters))
     early = permuted(early, straight)
     late = permuted(late, aside)
     halves = slice(0, half), slice(half, 2 * half)
-    earlier = [permuted(cur[:, lanes], [(i, i + 1) for i in near]) for lanes in halves]
-    later = [permuted(grad[:, lanes], [(i + 1, i) for i in near]) for lanes in halves]
+    earlier = [permuted(cur_next[:, lanes], [(i, i + 1) for i in near]) for lanes in halves]
+    later = [permuted(grad_next[:, lanes], [(i + 1, i) for i in near]) for lanes in halves]
     matrices = circulants(filters)
     late = lax.optimization_barrier(jnp.where((x == 0) | last, jnp.zeros_like(late), late))
     late = permuted(jnp.where((x == 0) | last, jnp.zeros_like(late), late), onward)

time: 125 us -> 130 us (1.040)
  the two profiles are of different devices: /device:TPU:1 before, /device:TPU:10 now
where the time goes in v5:
time: 130 us; the launch traced here: 129 us
  starting transfers between devices  31.3 us (24%)
  blocking collectives  29.1 us (22%)
  waiting for transfers between devices  28.3 us (22%)
  Pallas kernels  20 us (15%)
  local copies, waits for them, and re-layouts  12.8 us (10%)
  other arithmetic  7.14 us (5%)
    ppermute x8, starting transfers between devices, permuted(): return lax.ppermute(array, 'ctx', pairs)  31.3 us
    ppermute x8, waiting for transfers between devices, permuted(): return lax.ppermute(array, 'ctx', pairs)  28.3 us
    all_to_all x1, blocking collectives, over_column(): lax.all_to_all(sent, ('dp', 'ctx'), 0, 0, axis_index_groups=columns, tile...  17.7 us
    all_to_all x1, blocking collectives, over_plane(): lax.all_to_all(sent, 'ctx', 0, 0, axis_index_groups=pairs, tiled=True)  11.4 us
    pallas_call x1, Pallas kernels, main_part(): pl.pallas_call(main_kernel, grid_spec=pltpu.PrefetchScalarGridSpec(num_sc...  11.1 us
    unnamed x12, local copies, waits for them, and re-layouts  6.62 us
    pallas_call x2, Pallas kernels, far_fix(): pl.pallas_call(far_fix_kernel, grid_spec=pltpu.PrefetchScalarGridSpec(num...  4.88 us
    pallas_call x1, Pallas kernels, circulants(): pl.pallas_call(circulant_kernel, grid=(groups // step,), in_specs=[pl.Blo...  3.99 us
  transfers between devices with their start and end apart: 8, of which 5 were waited for; matrix products, arithmetic and copies ran while one was open for 7% of the time, Pallas kernels for 13%

profile of v5, /device:TPU:10, one launch (start us, length us, event | category | flops | bytes accessed | tf_op | source)
XLA Modules:
  0.0 129.4 jit_solution(17532262470561311280)
XLA Ops:
  0.7 2.1 %slice_select_fusion = bf16[128,2048]{1,0:T(8,128)(2,1)} fusion(bf16[128,4096]{1,0:T(8,128)(2,1)} %bitcast.18, bf16[128,4096]{1,0:T(8,128)(2,1)} %bitcast.25, pred[]{:T(512)S(6)} %eq.10), kind=kLoop, calls=%fused_computation.2 | loop fusion | flops 262144 | bytes 1572865 | tf_op jit(solution)/shard_map/jit(_where)/select_n | solution.py:335
  2.7 2.2 %slice_select_fusion.1 = bf16[128,2048]{1,0:T(8,128)(2,1)} fusion(bf16[128,4096]{1,0:T(8,128)(2,1)} %bitcast.19, bf16[128,4096]{1,0:T(8,128)(2,1)} %bitcast.26, pred[]{:T(512)S(6)} %eq.10), kind=kLoop, calls=%fused_computation.3 | loop fusion | flops 262144 | bytes 1572865 | tf_op jit(solution)/shard_map/jit(_where)/select_n | solution.py:337
  5.7 1.3 collective-permute-start
  7.0 2.3 %fusion.1 = (bf16[128,2048]{1,0:T(8,128)(2,1)}, bf16[128,2048]{1,0:T(8,128)(2,1)}) fusion(bf16[128,4096]{1,0:T(8,128)(2,1)} %bitcast.27), kind=kLoop, calls=%fused_computation.9 | loop fusion | bytes 2097152 | tf_op jit(solution)/shard_map/slice | solution.py:342
  9.2 3.4 %collective-permute-start.4 = (bf16[128,2048]{1,0:T(8,128)(2,1)}, bf16[128,2048]{1,0:T(8,128)(2,1)S(1)}, u32[]{:S(2)}, u32[]{:S(2)}) collective-permute-start(bf16[128,2048]{1,0:T(8,128)(2,1)} %get-tuple-element.59), channel_id=1, source_target_pairs={{0,1},{1,2},{2,3},{4,5},{5,6},{6,7},{8,9},{9,10},{10,11},{12,13},{... | collective-permute-start | bytes 1572872 | tf_op jit(solution)/shard_map/ppermute | solution.py:316
  12.6 18.9 %collective-permute-start.3 = (bf16[128,2048]{1,0:T(8,128)(2,1)}, bf16[128,2048]{1,0:T(8,128)(2,1)}, u32[]{:S(2)}, u32[]{:S(2)}) collective-permute-start(bf16[128,2048]{1,0:T(8,128)(2,1)} %get-tuple-element.60), channel_id=1, source_target_pairs={{0,1},{1,2},{2,3},{4,5},{5,6},{6,7},{8,9},{9,10},{10,11},{12,13},{... | collective-permute-start | bytes 1572872 | tf_op jit(solution)/shard_map/ppermute | solution.py:316
  31.5 2.3 %fusion = (bf16[128,2048]{1,0:T(8,128)(2,1)}, bf16[128,2048]{1,0:T(8,128)(2,1)}) fusion(bf16[128,4096]{1,0:T(8,128)(2,1)} %bitcast.20), kind=kLoop, calls=%fused_computation.8 | loop fusion | bytes 2097152 | tf_op jit(solution)/shard_map/slice | solution.py:343
  33.9 1.9 %collective-permute-start.6 = (bf16[128,2048]{1,0:T(8,128)(2,1)}, bf16[128,2048]{1,0:T(8,128)(2,1)}, u32[]{:S(2)}, u32[]{:S(2)}) collective-permute-start(bf16[128,2048]{1,0:T(8,128)(2,1)} %get-tuple-element.57), channel_id=1, source_target_pairs={{1,0},{2,1},{3,2},{5,4},{6,5},{7,6},{9,8},{10,9},{11,10},{13,12},{... | collective-permute-start | bytes 1572872 | tf_op jit(solution)/shard_map/ppermute | solution.py:316
  35.8 1.9 %collective-permute-done = bf16[128,2048]{1,0:T(8,128)(2,1)} collective-permute-done((bf16[128,2048]{1,0:T(8,128)(2,1)}, bf16[128,2048]{1,0:T(8,128)(2,1)}, u32[]{:S(2)}, u32[]{:S(2)}) %collective-permute-start) | collective-permute-done | bytes 524320 | tf_op jit(solution)/shard_map/ppermute | solution.py:316
  37.7 1.9 %collective-permute-start.5 = (bf16[128,2048]{1,0:T(8,128)(2,1)}, bf16[128,2048]{1,0:T(8,128)(2,1)}, u32[]{:S(2)}, u32[]{:S(2)}) collective-permute-start(bf16[128,2048]{1,0:T(8,128)(2,1)} %get-tuple-element.58), channel_id=1, source_target_pairs={{1,0},{2,1},{3,2},{5,4},{6,5},{7,6},{9,8},{10,9},{11,10},{13,12},{... | collective-permute-start | bytes 1572872 | tf_op jit(solution)/shard_map/ppermute | solution.py:316
  41.6 7.3 %collective-permute-done.4.earlier_hi_ref = bf16[128,2048]{1,0:T(8,128)(2,1)S(1)} collective-permute-done((bf16[128,2048]{1,0:T(8,128)(2,1)}, bf16[128,2048]{1,0:T(8,128)(2,1)S(1)}, u32[]{:S(2)}, u32[]{:S(2)}) %collective-permute-start.4) | collective-permute-done | bytes 524320 | tf_op jit(solution)/shard_map/ppermute | solution.py:316
  48.8 1.9 %collective-permute-start.1 = (bf16[128,2048]{1,0:T(8,128)(2,1)}, bf16[128,2048]{1,0:T(8,128)(2,1)}, u32[]{:S(2)}, u32[]{:S(2)}) collective-permute-start(bf16[128,2048]{1,0:T(8,128)(2,1)} %broadcast_select_fusion), channel_id=1, source_target_pairs={{2,5},{6,9},{10,13},{14,17},{18,21},{22,25},{26,29},{5,2},{9,6},{1... | collective-permute-start | bytes 1572872 | tf_op jit(solution)/shard_map/ppermute | solution.py:316
  50.7 4.0 %circulants.1 = bf16[2,256,64,128]{3,2,1,0:T(8,128)(2,1)S(1)} custom-call(bf16[256,128]{1,0:T(8,128)(2,1)S(1)} %copy-done.5), custom_call_target="tpu_custom_call" | custom-call | flops 1 | bytes 1 | tf_op jit(solution)/shard_map/circulants/pallas_call | solution.py:53
  54.8 3.2 %copy-done = bf16[2,256,64,128]{3,2,1,0:T(8,128)(2,1)} copy-done((bf16[2,256,64,128]{3,2,1,0:T(8,128)(2,1)}, bf16[2,256,64,128]{3,2,1,0:T(8,128)(2,1)S(1)}, u32[]{:S(2)}) %copy-start) | copy-done | bytes 8388632
  60.1 3.4 %copy-done.1 = bf16[2,256,64,128]{3,2,1,0:T(8,128)(2,1)S(1)} copy-done((bf16[2,256,64,128]{3,2,1,0:T(8,128)(2,1)S(1)}, bf16[2,256,64,128]{3,2,1,0:T(8,128)(2,1)}, u32[]{:S(2)}) %copy-start.1) | copy-done | bytes 8388632
  63.5 11.1 %main_part.1 = (bf16[128,4096]{1,0:T(8,128)(2,1)}, bf16[128,4096]{1,0:T(8,128)(2,1)}, f32[256,128]{1,0:T(8,128)S(1)}, f32[1,4096]{1,0:T(1,128)S(1)}) custom-call(s32[1]{0:T(128)} %bitcast.4.place_ref, bf16[128,2048]{1,0:T(8,128)(2,1)} %collective-permute-done.3.earlier_lo_ref, bf16[128,2048]{1,0:T(8,128)(2,1)S(1)} %collective-permute-done.4.earlier_hi_ref, ...), custom_call_target="tpu_custom_call" | custom-call | flops 1 | bytes 1 | tf_op jit(solution)/shard_map/main_part/pallas_call | solution.py:166
  74.6 2.1 %early_fix.1 = (bf16[128,4096]{1,0:T(8,128)(2,1)}, bf16[128,4096]{1,0:T(8,128)(2,1)}, f32[256,128]{1,0:T(8,128)S(1)}) custom-call(s32[1]{0:T(128)} %bitcast.4.place_ref, bf16[128,2048]{1,0:T(8,128)(2,1)S(1)} %collective-permute-done.2.halo_ref, bf16[128,4096]{1,0:T(8,128)(2,1)S(1)} %bitcast.29, ...), custom_call_target="tpu_custom_call", output_to_operand_aliasing={{0}: (7, {}), {1}: (8, {}), {2}: (11, {})} | custom-call | flops 1 | bytes 1 | tf_op jit(solution)/shard_map/early_fix/pallas_call | solution.py:274
  76.8 12.6 %conditional.2 = (f32[32,72]{1,0:T(8,128)S(1)}) conditional(s32[]{:T(128)} %convert_element_type.4, () %tuple.25, (f32[256,128]{1,0:T(8,128)S(1)}, f32[1,4096]{1,0:T(1,128)S(1)}) %tuple.28), branch_computations={%region_0.1_spmd, %region_1.3_spmd} | conditional | flops 73728 | bytes 1721356 | solution.py:312
  77.3 11.4 %all_to_all.15 = f32[16,1,2304]{2,1,0:T(1,128)S(1)} all-to-all(f32[16,1,2304]{2,1,0:T(1,128)S(1)} %all_to_all.12), channel_id=1, replica_groups={{0,1,2,3,8,9,10,11,16,17,18,19,24,25,26,27},{4,5,6,7,12,13,14,15,20,21,..., dimensions={0} | all-to-all | bytes 294912 | tf_op jit(solution)/shard_map/cond/branch_1_fun/all_to_all | solution.py:292
  89.4 17.0 %collective-permute-done.1 = bf16[128,2048]{1,0:T(8,128)(2,1)} collective-permute-done((bf16[128,2048]{1,0:T(8,128)(2,1)}, bf16[128,2048]{1,0:T(8,128)(2,1)}, u32[]{:S(2)}, u32[]{:S(2)}) %collective-permute-start.1) | collective-permute-done | bytes 524320 | tf_op jit(solution)/shard_map/ppermute | solution.py:316
  106.3 1.3 %collective-permute-start.7 = (bf16[128,2048]{1,0:T(8,128)(2,1)}, bf16[128,2048]{1,0:T(8,128)(2,1)S(1)}, u32[]{:S(2)}, u32[]{:S(2)}) collective-permute-start(bf16[128,2048]{1,0:T(8,128)(2,1)} %collective-permute-done.1), channel_id=1, source_target_pairs={{5,4},{9,8},{13,12},{17,16},{21,20},{25,24},{29,28},{2,3},{6,7},{1... | collective-permute-start | bytes 1572872 | tf_op jit(solution)/shard_map/ppermute | solution.py:316
  107.6 17.7 %conditional.3 = (f32[72]{0:T(128)S(1)}) conditional(s32[]{:T(128)} %convert_element_type.4, () %tuple.30, f32[32,72]{1,0:T(8,128)S(1)} %get-tuple-element.61), branch_computations={%region_3.4_spmd, %region_4.6_spmd} | conditional | flops 2232 | bytes 27948 | solution.py:312
  107.6 17.7 %all_to_all.16 = f32[32,1,72]{2,1,0:T(1,128)S(1)} all-to-all(f32[32,1,72]{2,1,0:T(1,128)S(1)} %bitcast.40), channel_id=1, replica_groups={{0,32,64,96,128,160,192,224,256,288,320,352,384,416,448,480,4,36,68,100..., dimensions={0} | all-to-all | bytes 18432 | tf_op jit(solution)/shard_map/cond/branch_1_fun/all_to_all | solution.py:305
  126.6 2.7 %late_fix.1 = (bf16[128,4096]{1,0:T(8,128)(2,1)}, bf16[128,4096]{1,0:T(8,128)(2,1)}) custom-call(s32[1]{0:T(128)} %bitcast.4.place_ref, bf16[128,2048]{1,0:T(8,128)(2,1)S(1)} %collective-permute-done.7.halo_ref, bf16[128,4096]{1,0:T(8,128)(2,1)S(1)} %bitcast.31, bf16[128,4096]{1,0:T(8,128)(2,1)S(1)} %bitcast.24, ...), custom_call_target="tpu_custom_call", output_to_operand_aliasing={{0}: (7, {}), {1}: (8, {})} | custom-call | flops 1 | bytes 1 | tf_op jit(solution)/shard_map/late_fix/pallas_call | solution.py:274
  (37 shorter events, 7.2 us)
Async XLA Ops:
  0.6 50.1 %copy-start.5 = (bf16[256,128]{1,0:T(8,128)(2,1)S(1)}, bf16[256,128]{1,0:T(8,128)(2,1)}, u32[]{:S(2)}) copy-start(bf16[256,128]{1,0:T(8,128)(2,1)} %taps_ref) | copy-start | bytes 196612
  2.7 57.4 %copy-start.2 = (bf16[1,128,4096]{2,1,0:T(8,128)(2,1)S(1)}, bf16[1,128,4096]{2,1,0:T(8,128)(2,1)}, u32[]{:S(2)}) copy-start(bf16[1,128,4096]{2,1,0:T(8,128)(2,1)} %param.9) | copy-start | bytes 3145732
  2.7 57.4 %copy-start.3 = (bf16[1,128,4096]{2,1,0:T(8,128)(2,1)S(1)}, bf16[1,128,4096]{2,1,0:T(8,128)(2,1)}, u32[]{:S(2)}) copy-start(bf16[1,128,4096]{2,1,0:T(8,128)(2,1)} %param.8) | copy-start | bytes 3145732
  2.7 57.4 %copy-start.4 = (f32[4096]{0:T(1024)S(1)}, f32[4096]{0:T(1024)}, u32[]{:S(2)}) copy-start(f32[4096]{0:T(1024)} %param.11) | copy-start | bytes 49156
  5.0 69.7 %collective-permute-start.2 = (bf16[128,2048]{1,0:T(8,128)(2,1)}, bf16[128,2048]{1,0:T(8,128)(2,1)S(1)}, u32[]{:S(2)}, u32[]{:S(2)}) collective-permute-start(bf16[128,2048]{1,0:T(8,128)(2,1)} %slice_select_fusion.1), channel_id=1, source_target_pairs={{3,4},{7,8},{11,12},{15,16},{19,20},{23,24},{27,28},{4,3},{8,7},{1... | collective-permute-start | bytes 1572872 | tf_op jit(solution)/shard_map/ppermute | solution.py:316
  5.7 32.0 %collective-permute-start = (bf16[128,2048]{1,0:T(8,128)(2,1)}, bf16[128,2048]{1,0:T(8,128)(2,1)}, u32[]{:S(2)}, u32[]{:S(2)}) collective-permute-start(bf16[128,2048]{1,0:T(8,128)(2,1)} %slice_select_fusion), channel_id=1, source_target_pairs={{3,2},{7,6},{11,10},{15,14},{19,18},{23,22},{27,26},{4,5},{8,9},{1... | collective-permute-start | bytes 1572872 | tf_op jit(solution)/shard_map/ppermute | solution.py:316
  9.2 39.6 %collective-permute-start.4 = (bf16[128,2048]{1,0:T(8,128)(2,1)}, bf16[128,2048]{1,0:T(8,128)(2,1)S(1)}, u32[]{:S(2)}, u32[]{:S(2)}) collective-permute-start(bf16[128,2048]{1,0:T(8,128)(2,1)} %get-tuple-element.59), channel_id=1, source_target_pairs={{0,1},{1,2},{2,3},{4,5},{5,6},{6,7},{8,9},{9,10},{10,11},{12,13},{... | collective-permute-start | bytes 1572872 | tf_op jit(solution)/shard_map/ppermute | solution.py:316
  12.6 46.4 %collective-permute-start.3 = (bf16[128,2048]{1,0:T(8,128)(2,1)}, bf16[128,2048]{1,0:T(8,128)(2,1)}, u32[]{:S(2)}, u32[]{:S(2)}) collective-permute-start(bf16[128,2048]{1,0:T(8,128)(2,1)} %get-tuple-element.60), channel_id=1, source_target_pairs={{0,1},{1,2},{2,3},{4,5},{5,6},{6,7},{8,9},{9,10},{10,11},{12,13},{... | collective-permute-start | bytes 1572872 | tf_op jit(solution)/shard_map/ppermute | solution.py:316
  33.9 25.2 %collective-permute-start.6 = (bf16[128,2048]{1,0:T(8,128)(2,1)}, bf16[128,2048]{1,0:T(8,128)(2,1)}, u32[]{:S(2)}, u32[]{:S(2)}) collective-permute-start(bf16[128,2048]{1,0:T(8,128)(2,1)} %get-tuple-element.57), channel_id=1, source_target_pairs={{1,0},{2,1},{3,2},{5,4},{6,5},{7,6},{9,8},{10,9},{11,10},{13,12},{... | collective-permute-start | bytes 1572872 | tf_op jit(solution)/shard_map/ppermute | solution.py:316
  37.7 22.4 %collective-permute-start.5 = (bf16[128,2048]{1,0:T(8,128)(2,1)}, bf16[128,2048]{1,0:T(8,128)(2,1)}, u32[]{:S(2)}, u32[]{:S(2)}) collective-permute-start(bf16[128,2048]{1,0:T(8,128)(2,1)} %get-tuple-element.58), channel_id=1, source_target_pairs={{1,0},{2,1},{3,2},{5,4},{6,5},{7,6},{9,8},{10,9},{11,10},{13,12},{... | collective-permute-start | bytes 1572872 | tf_op jit(solution)/shard_map/ppermute | solution.py:316
  48.8 57.5 %collective-permute-start.1 = (bf16[128,2048]{1,0:T(8,128)(2,1)}, bf16[128,2048]{1,0:T(8,128)(2,1)}, u32[]{:S(2)}, u32[]{:S(2)}) collective-permute-start(bf16[128,2048]{1,0:T(8,128)(2,1)} %broadcast_select_fusion), channel_id=1, source_target_pairs={{2,5},{6,9},{10,13},{14,17},{18,21},{22,25},{26,29},{5,2},{9,6},{1... | collective-permute-start | bytes 1572872 | tf_op jit(solution)/shard_map/ppermute | solution.py:316
  54.7 3.2 %copy-start = (bf16[2,256,64,128]{3,2,1,0:T(8,128)(2,1)}, bf16[2,256,64,128]{3,2,1,0:T(8,128)(2,1)S(1)}, u32[]{:S(2)}) copy-start(bf16[2,256,64,128]{3,2,1,0:T(8,128)(2,1)S(1)} %circulants.1) | copy-start | bytes 25165828
  60.1 3.4 %copy-start.1 = (bf16[2,256,64,128]{3,2,1,0:T(8,128)(2,1)S(1)}, bf16[2,256,64,128]{3,2,1,0:T(8,128)(2,1)}, u32[]{:S(2)}) copy-start(bf16[2,256,64,128]{3,2,1,0:T(8,128)(2,1)} %copy-done) | copy-start | bytes 25165828
  106.3 20.3 %collective-permute-start.7 = (bf16[128,2048]{1,0:T(8,128)(2,1)}, bf16[128,2048]{1,0:T(8,128)(2,1)S(1)}, u32[]{:S(2)}, u32[]{:S(2)}) collective-permute-start(bf16[128,2048]{1,0:T(8,128)(2,1)} %collective-permute-done.1), channel_id=1, source_target_pairs={{5,4},{9,8},{13,12},{17,16},{21,20},{25,24},{29,28},{2,3},{6,7},{1... | collective-permute-start | bytes 1572872 | tf_op jit(solution)/shard_map/ppermute | solution.py:316
